TPU v7x, 512 devices: a whole 4x4x16 slice. The times are simulated.
512 devices in a mesh: seq: 16 (over z), vocab: 8 (over y, core), rep: 4 (over x).
Axes of the slice: x: 4, y: 4, z: 16, core: 2. Of those that a mesh axis runs over, the one named last changes fastest.
Arguments:
- hidden: bfloat16 [4, 1024, 4096], P('rep', 'seq', 'vocab'), may hold values from -128 to 128
- head_weight: bfloat16 [4096, 81920], P('vocab', ('seq', 'rep')), may hold values from -0.25 to 0.25
- positions: int32 [4, 64], replicated, may hold values from 0 to 1023, as said below
- counts: int32 [4], replicated, may hold values from 48 to 64, as said below
- targets: int32 [4, 64], replicated, may hold values from 0 to 81919
- seq_cotangent: float32 [4], replicated, may hold values from 50 to 500
Outputs:
- grad_head: bfloat16 [4096, 81920], P('vocab', ('seq', 'rep'))
- grad_hidden: bfloat16 [4, 1024, 4096], P('rep', 'seq', 'vocab')
- seq_losses: float32 [4], replicated
Inputs may be any that keep to these rules, and one draw needn't show every extreme that they name: For each sequence the first counts entries are distinct positions in ascending order and the others are 0; at most 12 of a sequence's masked positions lie in one block of 64 consecutive positions, and in every sequence some block holds exactly 12. `counts`: some sequence has exactly 64 masked positions.
All inputs are finite; a program needn't handle non-finite values.
Results may differ from a plain program's by a relative error of at most 0.0047.
Values may be sent and summed in bfloat16 or wider, within the bound.
A program may use at most 64 MiB of HBM per device.

v0:
```python
import jax
import jax.numpy as jnp
from jax import lax
from jax.sharding import PartitionSpec as P

MASK_DEV = 4


def pick(table, lookup):
    table_size = table.shape[0]
    matches = lookup[..., None] == jnp.arange(table_size, dtype=jnp.int32)
    return jnp.sum(jnp.where(matches, table, jnp.zeros((), table.dtype)), axis=-1)


def softmax_grad(logits, row_target, row_weight, column_start):
    columns = column_start + jnp.arange(logits.shape[1], dtype=jnp.int32)
    is_target = columns[None, :] == row_target[:, None]
    target_part = jnp.sum(jnp.where(is_target, logits, 0.0), axis=1)
    row_max = lax.pmax(jnp.max(logits, axis=1), ("seq", "rep"))
    exponent = jnp.exp(logits - row_max[:, None])
    exp_total, target_logit = lax.psum((jnp.sum(exponent, axis=1), target_part), ("seq", "rep"))
    grad_logits = (
        row_weight[:, None] * (exponent / exp_total[:, None] - is_target.astype(jnp.float32))
    ).astype(jnp.bfloat16)
    row_loss = jnp.log(exp_total) + row_max - target_logit
    return (grad_logits, row_loss)


def losses_by_seq(row_loss, row_live, row_seq, count_rows, seq_total):
    per_row = jnp.where(row_live, row_loss / count_rows, 0.0)
    owners = row_seq[:, None] == jnp.arange(seq_total, dtype=jnp.int32)[None, :]
    return jnp.sum(jnp.where(owners, per_row[:, None], 0.0), axis=0)


def shards(hidden, head_weight, positions, counts, targets, seq_cotangent):
    seq_count = lax.axis_size("seq")
    rep_count = lax.axis_size("rep")
    seq_index = lax.axis_index("seq")
    rep_index = lax.axis_index("rep")
    seq_total = counts.shape[0]
    mask_cap = positions.shape[1]
    tok_dev = hidden.shape[1]
    features = hidden.shape[2]
    local_hidden = hidden[0]
    stride = seq_count + 1
    bounds = jnp.arange(stride, dtype=jnp.int32) * tok_dev
    slot_live = jnp.arange(mask_cap, dtype=jnp.int32)[None, :] < counts[:, None]
    below = slot_live[:, :, None] & (positions[:, :, None] < bounds[None, None, :])
    row_edges = jnp.sum(below.astype(jnp.int32), axis=1).reshape(-1)
    row_pos = lax.dynamic_index_in_dim(positions, rep_index, 0, keepdims=False)
    first_row = pick(row_edges, rep_index * stride + seq_index)
    last_row = pick(row_edges, rep_index * stride + seq_index + 1)
    flat_targets = targets.reshape(-1)
    scale_seq = seq_cotangent / counts.astype(jnp.float32)
    per_device = 3 * MASK_DEV
    slot_ids = first_row + jnp.arange(per_device, dtype=jnp.int32)
    own_live = slot_ids < last_row
    local_pos = pick(row_pos, jnp.clip(slot_ids, 0, mask_cap - 1)) - seq_index * tok_dev
    picked_rows = jnp.take(local_hidden, jnp.clip(local_pos, 0, tok_dev - 1), axis=0)
    picked_rows = jnp.where(own_live[:, None], picked_rows, jnp.zeros((), jnp.bfloat16))
    gathered = lax.all_gather(picked_rows, ("seq", "rep"), axis=0, tiled=True)
    gathered_ids = jnp.arange(gathered.shape[0], dtype=jnp.int32)
    src_seq = gathered_ids // (rep_count * per_device)
    src_rep = gathered_ids // per_device % rep_count
    edge_at = src_rep * stride + src_seq
    slot_k = pick(row_edges, edge_at) + gathered_ids % per_device
    row_live = slot_k < pick(row_edges, edge_at + 1)
    row_target = pick(flat_targets, src_rep * mask_cap + jnp.clip(slot_k, 0, mask_cap - 1))
    row_weight = jnp.where(row_live, pick(scale_seq, src_rep), 0.0)
    count_rows = pick(counts, src_rep).astype(jnp.float32)
    column_start = (seq_index * rep_count + rep_index) * head_weight.shape[1]
    partial_value = jnp.dot(gathered, head_weight, preferred_element_type=jnp.float32)
    logits = lax.psum(partial_value, "vocab")
    grad_logits, row_loss = softmax_grad(logits, row_target, row_weight, column_start)
    seq_losses = losses_by_seq(row_loss, row_live, src_rep, count_rows, seq_total)
    grad_head = lax.dot_general(
        gathered, grad_logits, (((0,), (0,)), ((), ())), preferred_element_type=jnp.float32
    ).astype(jnp.bfloat16)
    my_rows = lax.psum_scatter(
        lax.dot_general(
            grad_logits, head_weight, (((1,), (1,)), ((), ())), preferred_element_type=jnp.float32
        ),
        ("seq", "rep"),
        scatter_dimension=0,
        tiled=True,
    ).astype(jnp.bfloat16)
    grad_local = jnp.zeros((tok_dev, features), jnp.bfloat16)
    target_idx = jnp.where(own_live, local_pos, tok_dev)
    grad_local = grad_local.at[target_idx].add(my_rows, mode="drop")
    return (grad_head, grad_local[None], seq_losses)


def solution(mesh):
    return jax.shard_map(
        shards,
        mesh=mesh,
        in_specs=(P("rep", "seq", "vocab"), P("vocab", ("seq", "rep")), P(), P(), P(), P()),
        out_specs=(P("vocab", ("seq", "rep")), P("rep", "seq", "vocab"), P()),
        check_vma=False,
    )
```

profile of v0, /device:TPU:2, one launch (start us, length us, event | category | flops | bytes accessed | tf_op | source)
XLA Modules:
  0.0 726.8 jit_solution(2084206906965458476)
XLA Ops:
  7.2 0.8 iota_compare_fusion.5
  8.1 1.1 convert_reduce_fusion
  9.2 0.6 select_reduce_fusion.6
  9.8 0.6 fusion.25
  10.5 0.7 dynamic-slice_bitcast_fusion
  11.2 0.2 select_reduce_fusion.8
  11.4 1.3 compare_and_fusion
  12.7 1.3 fusion.24
  14.0 1.4 gather_fusion
  15.5 106.8 %all-gather = bf16[64,12,512]{2,1,0:T(8,128)(2,1)S(1)} all-gather(bf16[1,12,512]{2,1,0:T(8,128)(2,1)S(1)} %select_bitcast_fusion), channel_id=1, replica_groups=mesh['seq'=16,'vocab'=8,'rep'=4] {'seq','rep'}, dimensions={0}, use_global_device_ids=true | all-gather | bytes 798720 | tf_op jit(solution)/shard_map/all_gather | solution.py:61
  122.3 0.2 reshape.187
  122.6 3.1 fusion.28
  125.7 0.1 copy.9
  125.8 0.1 reshape.168
  125.8 0.1 reshape.169
  126.0 0.1 select_reduce_fusion.4
  126.1 0.1 select_reduce_fusion.2
  126.2 0.3 select_reduce_fusion
  126.6 82.4 %all-reduce.5.cloned.1.call-done = f32[768,1280]{1,0:T(8,128)} async-done(((f32[768,1280]{1,0:T(8,128)}), f32[768,1280]{1,0:T(8,128)}) %all-reduce.5.cloned.1.call-update) | async-done | bytes 3932176 | tf_op jit(solution)/shard_map/psum | solution.py:73
  208.9 2.4 reduce_max.9
  211.3 140.2 %pmax.7 = f32[768]{0:T(1024)S(1)} all-reduce(f32[768]{0:T(1024)S(1)} %reduce_max.9), channel_id=1, replica_groups=mesh['seq'=16,'vocab'=8,'rep'=4] {'seq','rep'}, use_global_device_ids=true, to_apply=%region_9.10 | all-reduce | flops 768 | bytes 6144 | tf_op jit(solution)/shard_map/pmax | solution.py:19
  351.5 2.9 fusion.4
  354.3 144.6 %all-reduce.2 = (f32[768]{0:T(1024)S(1)}, f32[768]{0:T(1024)S(1)}) all-reduce(f32[768]{0:T(1024)S(1)} %get-tuple-element.4, f32[768]{0:T(1024)S(1)} %get-tuple-element.3), channel_id=1, replica_groups=mesh['seq'=16,'vocab'=8,'rep'=4] {'seq','rep'}, use_global_device_ids=true, to_apply=%region_11.12 | all-reduce | flops 1536 | bytes 12288 | tf_op jit(solution)/shard_map/psum | solution.py:21
  498.9 0.6 select_reduce_fusion.3
  499.6 2.9 fusion.3
  502.5 1.3 copy-done.1
  503.8 2.3 fusion.29
  506.1 151.8 %fusion = f32[16,512]{1,0:T(8,128)S(1)} fusion(f32[768,512]{1,0:T(8,128)} %fusion.29), kind=kCustom, calls=%all-reduce-scatter | all-reduce-scatter fusion | flops 524289 | bytes 1607680
  658.0 4.4 collective-permute-start.15
  662.4 1.9 collective-permute-start
  664.3 1.3 collective-permute-start.1
  665.6 9.1 %collective-permute-start.10 = (f32[16,512]{1,0:T(8,128)S(1)}, f32[16,512]{1,0:T(8,128)S(1)}, u32[]{:S(2)}, u32[]{:S(2)}) collective-permute-start(f32[16,512]{1,0:T(8,128)S(1)} %fusion), channel_id=1, source_target_pairs={{0,67},{1,96},{2,97},{3,98},{32,99},{33,128},{34,129},{35,130},{64... | collective-permute-start | bytes 98312
  674.7 3.2 collective-permute-start.11
  677.9 2.8 collective-permute-start.12
  680.7 5.0 collective-permute-start.13
  685.7 4.0 collective-permute-start.14
  689.7 3.6 collective-permute-start.2
  693.4 2.0 collective-permute-start.3
  695.4 1.6 collective-permute-start.4
  697.0 1.3 dynamic-slice.4
  698.9 4.9 collective-permute-start.5
  703.8 1.3 collective-permute-start.6
  705.1 2.2 collective-permute-start.7
  707.3 3.1 collective-permute-start.8
  710.4 2.5 collective-permute-start.9
  712.9 3.8 convolution_convert_fusion
  716.8 1.9 concatenate
  718.7 1.3 scatter_custom_fusion
  (38 shorter events, 0.3 us)
Async XLA Ops:
  7.2 115.3 %copy-start = (bf16[512,1280]{1,0:T(8,128)(2,1)S(1)}, bf16[512,1280]{1,0:T(8,128)(2,1)}, u32[]{:S(2)}) copy-start(bf16[512,1280]{1,0:T(8,128)(2,1)} %param.7) | copy-start | bytes 3932164
  7.2 201.8 %all-reduce.5.cloned.1.call-start = ((), (), s32[]{:S(2)}) async-start(), calls=%async_computation | async-start | bytes 7864320 | tf_op jit(solution)/shard_map/psum | solution.py:73
  122.5 3.3 copy-start.2
  122.5 3.4 copy-start.3
  122.5 4.0 copy-start.4
  502.5 1.3 copy-start.1
  658.0 19.9 %collective-permute-start.15 = (f32[12,512]{1,0:T(8,128)S(1)}, f32[12,512]{1,0:T(8,128)S(1)}, u32[]{:S(2)}, u32[]{:S(2)}) collective-permute-start(f32[12,512]{1,0:T(8,128)S(1)} %slice.2), channel_id=1, source_target_pairs={{0,128},{1,129},{2,130},{3,131},{32,160},{33,161},{34,162},{35,163... | collective-permute-start | bytes 73736
  662.4 18.3 %collective-permute-start = (f32[16,512]{1,0:T(8,128)S(1)}, f32[16,512]{1,0:T(8,128)S(1)}, u32[]{:S(2)}, u32[]{:S(2)}) collective-permute-start(f32[16,512]{1,0:T(8,128)S(1)} %fusion), channel_id=1, source_target_pairs={{0,1},{1,2},{2,3},{3,32},{32,33},{33,34},{34,35},{35,64},{64,65},{... | collective-permute-start | bytes 98312
  664.3 21.3 %collective-permute-start.1 = (f32[16,512]{1,0:T(8,128)S(1)}, f32[16,512]{1,0:T(8,128)S(1)}, u32[]{:S(2)}, u32[]{:S(2)}) collective-permute-start(f32[16,512]{1,0:T(8,128)S(1)} %fusion), channel_id=1, source_target_pairs={{0,2},{1,3},{2,32},{3,33},{32,34},{33,35},{34,64},{35,65},{64,66},... | collective-permute-start | bytes 98312
  665.6 24.1 %collective-permute-start.10 = (f32[16,512]{1,0:T(8,128)S(1)}, f32[16,512]{1,0:T(8,128)S(1)}, u32[]{:S(2)}, u32[]{:S(2)}) collective-permute-start(f32[16,512]{1,0:T(8,128)S(1)} %fusion), channel_id=1, source_target_pairs={{0,67},{1,96},{2,97},{3,98},{32,99},{33,128},{34,129},{35,130},{64... | collective-permute-start | bytes 98312
  674.7 18.6 %collective-permute-start.11 = (f32[16,512]{1,0:T(8,128)S(1)}, f32[16,512]{1,0:T(8,128)S(1)}, u32[]{:S(2)}, u32[]{:S(2)}) collective-permute-start(f32[16,512]{1,0:T(8,128)S(1)} %fusion), channel_id=1, source_target_pairs={{0,96},{1,97},{2,98},{3,99},{32,128},{33,129},{34,130},{35,131},{6... | collective-permute-start | bytes 98312
  677.9 17.4 %collective-permute-start.12 = (f32[16,512]{1,0:T(8,128)S(1)}, f32[16,512]{1,0:T(8,128)S(1)}, u32[]{:S(2)}, u32[]{:S(2)}) collective-permute-start(f32[16,512]{1,0:T(8,128)S(1)} %fusion), channel_id=1, source_target_pairs={{0,97},{1,98},{2,99},{3,128},{32,129},{33,130},{34,131},{35,160},{... | collective-permute-start | bytes 98312
  680.7 18.2 %collective-permute-start.13 = (f32[16,512]{1,0:T(8,128)S(1)}, f32[16,512]{1,0:T(8,128)S(1)}, u32[]{:S(2)}, u32[]{:S(2)}) collective-permute-start(f32[16,512]{1,0:T(8,128)S(1)} %fusion), channel_id=1, source_target_pairs={{0,98},{1,99},{2,128},{3,129},{32,130},{33,131},{34,160},{35,161},... | collective-permute-start | bytes 98312
  685.7 18.1 %collective-permute-start.14 = (f32[16,512]{1,0:T(8,128)S(1)}, f32[16,512]{1,0:T(8,128)S(1)}, u32[]{:S(2)}, u32[]{:S(2)}) collective-permute-start(f32[16,512]{1,0:T(8,128)S(1)} %fusion), channel_id=1, source_target_pairs={{0,99},{1,128},{2,129},{3,130},{32,131},{33,160},{34,161},{35,162}... | collective-permute-start | bytes 98312
  689.7 15.3 %collective-permute-start.2 = (f32[16,512]{1,0:T(8,128)S(1)}, f32[16,512]{1,0:T(8,128)S(1)}, u32[]{:S(2)}, u32[]{:S(2)}) collective-permute-start(f32[16,512]{1,0:T(8,128)S(1)} %fusion), channel_id=1, source_target_pairs={{0,3},{1,32},{2,33},{3,34},{32,35},{33,64},{34,65},{35,66},{64,67}... | collective-permute-start | bytes 98312
  693.4 14.0 %collective-permute-start.3 = (f32[16,512]{1,0:T(8,128)S(1)}, f32[16,512]{1,0:T(8,128)S(1)}, u32[]{:S(2)}, u32[]{:S(2)}) collective-permute-start(f32[16,512]{1,0:T(8,128)S(1)} %fusion), channel_id=1, source_target_pairs={{0,32},{1,33},{2,34},{3,35},{32,64},{33,65},{34,66},{35,67},{64,96... | collective-permute-start | bytes 98312
  695.4 15.1 %collective-permute-start.4 = (f32[16,512]{1,0:T(8,128)S(1)}, f32[16,512]{1,0:T(8,128)S(1)}, u32[]{:S(2)}, u32[]{:S(2)}) collective-permute-start(f32[16,512]{1,0:T(8,128)S(1)} %fusion), channel_id=1, source_target_pairs={{0,33},{1,34},{2,35},{3,64},{32,65},{33,66},{34,67},{35,96},{64,97... | collective-permute-start | bytes 98312
  698.9 17.8 %collective-permute-start.5 = (f32[16,512]{1,0:T(8,128)S(1)}, f32[16,512]{1,0:T(8,128)S(1)}, u32[]{:S(2)}, u32[]{:S(2)}) collective-permute-start(f32[16,512]{1,0:T(8,128)S(1)} %fusion), channel_id=1, source_target_pairs={{0,34},{1,35},{2,64},{3,65},{32,66},{33,67},{34,96},{35,97},{64,98... | collective-permute-start | bytes 98312
  703.8 12.9 %collective-permute-start.6 = (f32[16,512]{1,0:T(8,128)S(1)}, f32[16,512]{1,0:T(8,128)S(1)}, u32[]{:S(2)}, u32[]{:S(2)}) collective-permute-start(f32[16,512]{1,0:T(8,128)S(1)} %fusion), channel_id=1, source_target_pairs={{0,35},{1,64},{2,65},{3,66},{32,67},{33,96},{34,97},{35,98},{64,99... | collective-permute-start | bytes 98312
  705.1 11.6 %collective-permute-start.7 = (f32[16,512]{1,0:T(8,128)S(1)}, f32[16,512]{1,0:T(8,128)S(1)}, u32[]{:S(2)}, u32[]{:S(2)}) collective-permute-start(f32[16,512]{1,0:T(8,128)S(1)} %fusion), channel_id=1, source_target_pairs={{0,64},{1,65},{2,66},{3,67},{32,96},{33,97},{34,98},{35,99},{64,12... | collective-permute-start | bytes 98312
  707.3 9.4 %collective-permute-start.8 = (f32[16,512]{1,0:T(8,128)S(1)}, f32[16,512]{1,0:T(8,128)S(1)}, u32[]{:S(2)}, u32[]{:S(2)}) collective-permute-start(f32[16,512]{1,0:T(8,128)S(1)} %fusion), channel_id=1, source_target_pairs={{0,65},{1,66},{2,67},{3,96},{32,97},{33,98},{34,99},{35,128},{64,1... | collective-permute-start | bytes 98312
  710.4 6.3 collective-permute-start.9
Sparse Core Ops, SparseCore 0:
  125.8 83.1 all-reduce.4
where the time goes:
time: 728 us; the launch traced here: 727 us
  blocking collectives  543 us (75%)
  waiting for transfers between devices  82.4 us (11%)
  starting transfers between devices  52.8 us (7%)
  other arithmetic  16.8 us (2%)
  between operations  15.1 us (2%)
  matrix products  9.24 us (1%)
    unnamed x1, blocking collectives  152 us
    psum x1, blocking collectives, softmax_grad(): lax.psum((jnp.sum(exponent, axis=1), target_part), ('seq', 'rep'))  145 us
    pmax x1, blocking collectives, softmax_grad(): row_max = lax.pmax(jnp.max(logits, axis=1), ('seq', 'rep'))  140 us
    all_gather x1, blocking collectives, shards(): gathered = lax.all_gather(picked_rows, ('seq', 'rep'), axis=0, tiled=True)  107 us
    psum x1, waiting for transfers between devices, shards(): logits = lax.psum(partial_value, 'vocab')  82.4 us
    unnamed x16, starting transfers between devices  52.8 us
  transfers between devices with their start and end apart: 17, of which 1 were waited for; matrix products, arithmetic and copies ran while one was open for 1% of the time, Pallas kernels for 0%

commit v1 on v0

v1 whole, which is shorter than its diff:
```python
import jax
import jax.numpy as jnp
from jax import lax
from jax.experimental import pallas as pl
from jax.experimental.pallas import tpu as pltpu
from jax.sharding import PartitionSpec as P

MESH = pl.DeviceIdType.MESH
F32 = jnp.float32
BF16 = jnp.bfloat16

SEQ = 16
REP = 4
SLOTS = 64
TOK = 64
FEAT = 512
COLS = 1280
FOLD = 16
CHUNK = 32
HALF = 16
WIDE = FEAT // 2

PICK_CLASS = 0
PICK_NEAR = 6
PICK_REP = 14
LOGIT_CORE = 20
LOGIT_Y = 24
STAT_SEQ = 30
STAT_REP = 45
GRAD_Y = 48
GRAD_CORE = 54
SCALE = 58
ROW_REP = 65
ROW_NEAR = 71
ROW_CLASS = 79
MESSAGES = 85


def iota(shape, dim):
    return lax.broadcasted_iota(jnp.int32, shape, dim)


def to_column(row, rows, shift=0):
    shape = (rows, row.shape[1])
    at = iota(shape, 1) == iota(shape, 0) + shift
    return jnp.sum(jnp.where(at, row, 0.0), axis=1, keepdims=True)


def to_row(column, shift):
    shape = (CHUNK, 128)
    at = iota(shape, 1) == iota(shape, 0) + shift
    return jnp.sum(jnp.where(at, column, 0.0), axis=0, keepdims=True)


def turn(row, shift):
    return pltpu.roll(row, 128 - shift, 1)


def between(row, first):
    lane = iota((1, 128), 1)
    return jnp.where((lane >= first) & (lane < first + CHUNK), row, 0.0)


def merge_stats(ref, parts):
    rows = [ref[i] for i in range(parts)]
    row_max = rows[0]
    for row in rows[1:]:
        row_max = jnp.maximum(row_max, row)
    row_sum = jnp.zeros((1, 128), F32)
    row_target = jnp.zeros((1, 128), F32)
    for row in rows:
        row_sum = row_sum + turn(row, CHUNK) * jnp.exp(row - row_max)
        row_target = row_target + row
    return row_max, row_sum, turn(row_target, 2 * CHUNK)


def pack_stats(row_max, row_sum, row_target):
    return (
        between(row_max, 0)
        + between(turn(row_sum, 128 - CHUNK), CHUNK)
        + between(turn(row_target, 128 - 2 * CHUNK), 2 * CHUNK)
    )


def fold_rows(rows):
    return (rows[0:16] + rows[16:32]) + (rows[32:48] + rows[48:64])


def unfold_rows(rows):
    return jnp.concatenate([rows, rows, rows, rows], axis=0)


def kernel(
    counts_hbm, cot_hbm, positions_hbm, targets_hbm, hidden_hbm, weight_hbm,
    head_hbm, grad_ref, losses_ref,
    counts_ref, cot_ref, positions_ref, targets_ref, hidden_ref, weight, pick_class, pick_own, pick_near, picked, picked_t, target_cols, target_rows,
    core_out, core_in, part, y_fwd, y_sum, y_direct, y_acc, logits_ref,
    stat_seq, stat_rep, scales, exps, grads,
    row_sums, row_out, row_in, near_out, near_in, class_out, class_in, head_out,
    send_sem, recv_sem, load_sem, head_sem,
):
    z = lax.axis_index("seq")
    v = lax.axis_index("vocab")
    x = lax.axis_index("rep")
    y = lax.div(v, 2)
    c = lax.rem(v, 2)
    cls = lax.rem(z, 4)
    member = lax.div(z, 4)

    def at_z(shift):
        return {"seq": lax.rem(z + shift + SEQ, SEQ)}

    def at_x(shift):
        return {"rep": lax.rem(x + shift, REP)}

    def y_plus(shift):
        return lax.rem(y + shift, 4)

    def at_y(shift):
        return {"vocab": y_plus(shift) * 2 + c}

    def load(number, src, dst):
        copy = pltpu.make_async_copy(src, dst, load_sem.at[number])
        copy.start()
        return copy

    loads = [
        load(0, positions_hbm, positions_ref),
        load(1, counts_hbm, counts_ref),
        load(2, hidden_hbm, hidden_ref),
        load(3, cot_hbm, cot_ref),
        load(4, targets_hbm, targets_ref),
        load(5, weight_hbm, weight),
    ]

    sibling = {"vocab": y * 2 + 1 - c}

    started = []

    def send(number, src, dst, device):
        copy = pltpu.make_async_remote_copy(
            src_ref=src,
            dst_ref=dst,
            send_sem=send_sem.at[number],
            recv_sem=recv_sem.at[number],
            device_id=device,
            device_id_type=MESH,
        )
        copy.start()
        started.append(copy)
        return copy

    barrier = pltpu.get_barrier_semaphore()
    friends = [at_z(s) for s in range(1, SEQ)] + [at_x(s) for s in (1, 2, 3)]
    friends += [{"vocab": lax.rem(v + s, 8)} for s in range(1, 8)]
    for friend in friends:
        pl.semaphore_signal(barrier, inc=1, device_id=friend, device_id_type=MESH)

    loads[0].wait()
    loads[1].wait()
    all_positions = positions_ref[...].astype(F32)
    position_row = jnp.sum(
        jnp.where(iota((REP, SLOTS), 0) == x, all_positions, 0.0), axis=0, keepdims=True
    )
    count = counts_ref[x]
    position_col = to_column(position_row, SLOTS).astype(jnp.int32)
    live_col = iota((SLOTS, 1), 0) < count
    owner_col = jnp.where(live_col, lax.div(position_col, TOK), -1)
    pick_at = (iota((SLOTS, TOK), 1) + z * TOK == position_col) & (iota((SLOTS, TOK), 0) < count)
    put_at = (iota((TOK, SLOTS), 0) + z * TOK == position_row.astype(jnp.int32)) & (
        iota((TOK, SLOTS), 1) < count
    )

    loads[2].wait()
    own_rows = jnp.dot(
        jnp.where(pick_at, 1.0, 0.0).astype(BF16), hidden_ref[0], preferred_element_type=F32
    )
    folded = fold_rows(own_rows).astype(BF16)
    for h in range(2):
        pick_class[h, member] = folded[:, h * WIDE : (h + 1) * WIDE]

    pl.semaphore_wait(barrier, len(friends))

    class_copies = [
        [
            send(
                PICK_CLASS + 3 * h + d - 1, pick_class.at[h, member], pick_class.at[h, member],
                at_z(4 * d),
            )
            for d in (1, 2, 3)
        ]
        for h in range(2)
    ]

    def send_near(number, src, dst):
        low, high = pl.ds(0, 32), pl.ds(32, 32)
        return [
            send(number, src, dst.at[0], at_z(1)),
            send(number + 1, src, dst.at[1], at_z(-1)),
            send(number + 2, src.at[low], dst.at[2, low], at_z(2)),
            send(number + 3, src.at[high], dst.at[2, high], at_z(-2)),
        ]

    loads[4].wait()
    all_targets = targets_ref[...].astype(F32)
    column = iota((CHUNK, COLS), 1) + (z * REP + x) * COLS
    for i in range(8):
        target_cols[i] = to_column(
            all_targets[i // 2 : i // 2 + 1], CHUNK, CHUNK * (i % 2)
        ).astype(jnp.int32)

    def head_at_targets(h):
        hot = [jnp.where(column == target_cols[i], 1.0, 0.0).astype(BF16) for i in range(8)]
        target_rows[h] = lax.dot_general(
            jnp.concatenate(hot, axis=0), weight[h * WIDE : (h + 1) * WIDE],
            (((1,), (1,)), ((), ())), preferred_element_type=F32,
        ).reshape(8, CHUNK, WIDE)

    loads[5].wait()
    head_at_targets(0)

    totals = []
    near_copies = []
    for h in range(2):
        for copy in class_copies[h]:
            copy.wait_recv()
        total = jnp.zeros((SLOTS, WIDE), F32)
        for j in range(4):
            block = unfold_rows(pick_class[h, j].astype(F32))
            total = total + jnp.where(owner_col == cls + 4 * j, block, 0.0)
        pick_own[h] = total.astype(BF16)
        near_copies.append(send_near(PICK_NEAR + 4 * h, pick_own.at[h], pick_near.at[h]))
        totals.append(total)
    head_at_targets(1)
    rep_copies = []
    for h in range(2):
        for copy in near_copies[h]:
            copy.wait_recv()
        total = totals[h]
        for i in range(3):
            total = total + pick_near[h, i].astype(F32)
        picked[h, x] = total.astype(BF16)
        rep_copies.append([
            send(PICK_REP + 3 * h + d - 1, picked.at[h, x], picked.at[h, x], at_x(d))
            for d in (1, 2, 3)
        ])

    def partial_logits(h, core):
        rows = picked[h, pl.ds(2 * core, 2)].reshape(2 * SLOTS, WIDE)
        return jnp.dot(
            rows, weight[h * WIDE : (h + 1) * WIDE], preferred_element_type=F32
        ).reshape(4, CHUNK, COLS)

    for copy in rep_copies[0]:
        copy.wait_recv()
    core_out[...] = partial_logits(0, 1 - c)
    part[...] = partial_logits(0, c)
    for copy in rep_copies[1]:
        copy.wait_recv()
    core_out[...] = core_out[...] + partial_logits(1, 1 - c)
    order = (2, 1, 3, 0)
    core_copies = [
        send(LOGIT_CORE + i, core_out.at[y_plus(s)], core_in.at[y_plus(s)], sibling)
        for i, s in enumerate(order)
    ]
    part[...] = part[...] + partial_logits(1, c)

    low, high = pl.ds(0, HALF), pl.ds(HALF, HALF)
    y_copies = []
    for i, s in enumerate(order):
        core_copies[i].wait_recv()
        at = y_plus(s)
        part[at] = part[at] + core_in[at]
        if s == 2:
            y_copies.append(send(LOGIT_Y, part.at[at, low], y_fwd.at[0], at_y(1)))
            y_copies.append(send(LOGIT_Y + 1, part.at[at, high], y_fwd.at[1], at_y(3)))
        if s == 1:
            y_copies.append(send(LOGIT_Y + 2, part.at[at, high], y_direct.at[1], at_y(1)))
        if s == 3:
            y_copies.append(send(LOGIT_Y + 3, part.at[at, low], y_direct.at[0], at_y(3)))
    for h in range(2):
        picked_t[h * WIDE : (h + 1) * WIDE] = picked[h].reshape(REP * SLOTS, WIDE).T
    y_copies[0].wait_recv()
    y_sum[0] = y_fwd[0] + part[y_plus(1), 0:HALF]
    y_copies.append(send(LOGIT_Y + 4, y_sum.at[0], y_acc.at[0], at_y(1)))
    y_copies[1].wait_recv()
    y_sum[1] = y_fwd[1] + part[y_plus(3), HALF:CHUNK]
    y_copies.append(send(LOGIT_Y + 5, y_sum.at[1], y_acc.at[1], at_y(3)))
    for copy in y_copies[2:]:
        copy.wait_recv()
    logits_ref[0:HALF] = part[y, 0:HALF] + (y_direct[0] + y_acc[0])
    logits_ref[HALF:CHUNK] = part[y, HALF:CHUNK] + (y_direct[1] + y_acc[1])

    loads[3].wait()
    my_seq = 2 * c + lax.div(y, 2)
    first_slot = lax.rem(y, 2) * CHUNK
    my_count = counts_ref[my_seq]
    my_cot = cot_ref[my_seq]
    my_chunk = 4 * c + y
    is_target = column == target_cols[my_chunk]
    logits = logits_ref[...]
    local_max = jnp.max(logits, axis=1, keepdims=True)
    exponent = jnp.exp(logits - local_max)

    exps[my_chunk] = jnp.where(is_target, 0.0, exponent).astype(BF16)
    mine = exps.at[my_chunk]
    before = exps.at[4 * c + y_plus(3)]
    after = exps.at[4 * c + y_plus(1)]
    up_low = send(GRAD_Y, mine.at[low], mine.at[low], at_y(1))
    down_high = send(GRAD_Y + 1, mine.at[high], mine.at[high], at_y(3))
    up_high = send(GRAD_Y + 2, mine.at[high], mine.at[high], at_y(1))
    down_low = send(GRAD_Y + 3, mine.at[low], mine.at[low], at_y(3))
    core_copies = [send(GRAD_CORE, mine, mine, sibling)]

    local_sum = jnp.sum(exponent, axis=1, keepdims=True)
    local_target = jnp.sum(jnp.where(is_target, logits, 0.0), axis=1, keepdims=True)
    max_row = to_row(local_max, 0)
    stat_seq[z] = max_row + to_row(local_sum, CHUNK) + to_row(local_target, 2 * CHUNK)
    seq_copies = [
        send(STAT_SEQ + d - 1, stat_seq.at[z], stat_seq.at[z], at_z(d)) for d in range(1, SEQ)
    ]

    up_low.wait_recv()
    up_again = send(GRAD_Y + 4, before.at[low], before.at[low], at_y(1))
    down_high.wait_recv()
    down_again = send(GRAD_Y + 5, after.at[high], after.at[high], at_y(3))
    up_high.wait_recv()
    core_copies.append(send(GRAD_CORE + 1, before, before, sibling))
    down_low.wait_recv()
    core_copies.append(send(GRAD_CORE + 2, after, after, sibling))

    for copy in seq_copies:
        copy.wait_recv()
    stat_rep[x] = pack_stats(*merge_stats(stat_seq, SEQ))
    copies = [send(STAT_REP + d - 1, stat_rep.at[x], stat_rep.at[x], at_x(d)) for d in (1, 2, 3)]
    up_again.wait_recv()
    down_again.wait_recv()
    across = exps.at[4 * c + y_plus(2)]
    core_copies.append(send(GRAD_CORE + 3, across, across, sibling))
    for copy in copies:
        copy.wait_recv()
    total_max, total_sum, target_logit = merge_stats(stat_rep, REP)

    lane = iota((1, 128), 1)
    live = (lane < CHUNK) & (lane + first_slot < my_count)
    count_row = jnp.full((1, 128), my_count.astype(F32), F32)
    weight_row = jnp.where(live, jnp.full((1, 128), my_cot, F32) / count_row, 0.0)
    factor = jnp.where(live, weight_row * (jnp.exp(max_row - total_max) / total_sum), 0.0)
    at_target = jnp.where(
        live, weight_row * (jnp.exp(target_logit - total_max) / total_sum - 1.0), 0.0
    )
    row_loss = jnp.where(live, (jnp.log(total_sum) + total_max - target_logit) / count_row, 0.0)
    scales[my_chunk] = pack_stats(factor, at_target, row_loss)
    scale_copies = [
        send(SCALE + d - 1, scales.at[my_chunk], scales.at[my_chunk], {"vocab": lax.rem(v + d, 8)})
        for d in range(1, 8)
    ]

    def head_times(core):
        block = exps[pl.ds(4 * core, 4)].reshape(4 * CHUNK, COLS)
        for h in range(2):
            row_sums[h, pl.ds(4 * core, 4)] = lax.dot_general(
                block, weight[h * WIDE : (h + 1) * WIDE], (((1,), (1,)), ((), ())),
                preferred_element_type=F32,
            ).reshape(4, CHUNK, WIDE)

    head_times(c)
    for copy in core_copies:
        copy.wait_recv()
    head_times(1 - c)
    for copy in scale_copies:
        copy.wait_recv()
    factors = [to_column(scales[i], CHUNK) for i in range(8)]
    at_targets = [
        to_column(scales[i], CHUNK, CHUNK).astype(BF16).astype(F32) for i in range(8)
    ]
    rep_copies = []
    for h in range(2):
        for i in range(8):
            rows = factors[i] * row_sums[h, i] + at_targets[i] * target_rows[h, i]
            row_sums[h, i] = rows
            row_out[h, i // 2, CHUNK * (i % 2) : CHUNK * (i % 2 + 1)] = rows.astype(BF16)
        rep_copies.append([
            send(
                ROW_REP + 3 * h + d - 1, row_out.at[h, lax.rem(x + d, REP)], row_in.at[h, d - 1],
                at_x(d),
            )
            for d in (1, 2, 3)
        ])
    for i in range(8):
        values = exps[i].astype(F32) * factors[i]
        grads[i] = jnp.where(column == target_cols[i], at_targets[i], values).astype(BF16)
    owns = [row_sums[h, pl.ds(2 * x, 2)].reshape(SLOTS, WIDE) for h in range(2)]

    def head_part(i):
        columns = pl.ds(i * 256, 256)
        tile = jnp.dot(
            picked_t[...], grads[:, :, columns].reshape(REP * SLOTS, 256), preferred_element_type=F32
        )
        head_out[:, columns] = tile.astype(BF16)
        copy = pltpu.make_async_copy(
            head_out.at[:, columns], head_hbm.at[:, columns], head_sem.at[i]
        )
        copy.start()
        return copy

    near_copies = []
    for h in range(2):
        for copy in rep_copies[h]:
            copy.wait_recv()
        for i in range(3):
            owns[h] = owns[h] + row_in[h, i].astype(F32)
        near_out[h] = owns[h].astype(BF16)
        near_copies.append(send_near(ROW_NEAR + 4 * h, near_out.at[h], near_in.at[h]))
    head_copies = [head_part(0), head_part(1), head_part(2)]
    mine_rows = []
    class_copies = []
    for h in range(2):
        for copy in near_copies[h]:
            copy.wait_recv()
        own = owns[h]
        for i in range(3):
            own = own + near_in[h, i].astype(F32)
        mine = jnp.zeros((FOLD, WIDE), F32)
        for j in range(4):
            block = fold_rows(jnp.where(owner_col == cls + 4 * j, own, 0.0))
            class_out[h, j] = block.astype(BF16)
            mine = jnp.where(member == j, block, mine)
        mine_rows.append(mine)
        class_copies.append([
            send(
                ROW_CLASS + 3 * h + d - 1, class_out.at[h, lax.rem(member + d, 4)],
                class_in.at[h, d - 1], at_z(4 * d),
            )
            for d in (1, 2, 3)
        ])
    head_copies += [head_part(3), head_part(4)]
    for q in range(REP):
        losses_ref[q] = jnp.sum(between(scales[2 * q] + scales[2 * q + 1], 2 * CHUNK))
    put = jnp.where(put_at, 1.0, 0.0).astype(BF16)
    for h in range(2):
        for copy in class_copies[h]:
            copy.wait_recv()
        mine = mine_rows[h]
        for i in range(3):
            mine = mine + class_in[h, i].astype(F32)
        final = unfold_rows(mine.astype(BF16).astype(F32))
        final = jnp.where(owner_col == z, final, 0.0).astype(BF16)
        grad_ref[0, :, h * WIDE : (h + 1) * WIDE] = jnp.dot(
            put, final, preferred_element_type=F32
        ).astype(BF16)

    for copy in started:
        copy.wait_send()
    for copy in head_copies:
        copy.wait()


def hand_over(
    head_in, hidden_in, losses_in, head_ref, hidden_ref, losses_ref,
    head, hidden, losses, in_sem, out_sem,
):
    rows = FEAT // 4
    moves = [(hidden_in, hidden, hidden_ref), (losses_in, losses, losses_ref)]
    for i in range(4):
        at = pl.ds(i * rows, rows)
        moves.append((head_in.at[at], head.at[at], head_ref.at[at]))
    loads = [pltpu.make_async_copy(m[0], m[1], in_sem.at[i]) for i, m in enumerate(moves)]
    stores = [pltpu.make_async_copy(m[1], m[2], out_sem.at[i]) for i, m in enumerate(moves)]
    for load in loads:
        load.start()
    for load, store in zip(loads, stores):
        load.wait()
        store.start()
    for store in stores:
        store.wait()


def shards(hidden, head_weight, positions, counts, targets, seq_cotangent):
    vmem = pl.BlockSpec(memory_space=pltpu.VMEM)
    smem = pl.BlockSpec(memory_space=pltpu.SMEM)
    hbm = pl.BlockSpec(memory_space=pltpu.HBM)
    shapes = (
        jax.ShapeDtypeStruct((FEAT, COLS), BF16),
        jax.ShapeDtypeStruct((1, TOK, FEAT), BF16),
        jax.ShapeDtypeStruct((REP,), F32),
    )
    limit = 60 * 1024 * 1024
    results = pl.pallas_call(
        kernel,
        out_shape=shapes,
        in_specs=[hbm] * 6,
        out_specs=(hbm, vmem, smem),
        scratch_shapes=[
            pltpu.SMEM((REP,), jnp.int32),
            pltpu.SMEM((REP,), F32),
            pltpu.VMEM((REP, SLOTS), jnp.int32),
            pltpu.VMEM((REP, SLOTS), jnp.int32),
            pltpu.VMEM((1, TOK, FEAT), BF16),
            pltpu.VMEM((FEAT, COLS), BF16),
            pltpu.VMEM((2, 4, FOLD, WIDE), BF16),
            pltpu.VMEM((2, SLOTS, WIDE), BF16),
            pltpu.VMEM((2, 3, SLOTS, WIDE), BF16),
            pltpu.VMEM((2, REP, SLOTS, WIDE), BF16),
            pltpu.VMEM((FEAT, REP * SLOTS), BF16),
            pltpu.VMEM((8, CHUNK, 1), jnp.int32),
            pltpu.VMEM((2, 8, CHUNK, WIDE), F32),
            pltpu.VMEM((4, CHUNK, COLS), F32),
            pltpu.VMEM((4, CHUNK, COLS), F32),
            pltpu.VMEM((4, CHUNK, COLS), F32),
            pltpu.VMEM((2, HALF, COLS), F32),
            pltpu.VMEM((2, HALF, COLS), F32),
            pltpu.VMEM((2, HALF, COLS), F32),
            pltpu.VMEM((2, HALF, COLS), F32),
            pltpu.VMEM((CHUNK, COLS), F32),
            pltpu.VMEM((SEQ, 1, 128), F32),
            pltpu.VMEM((REP, 1, 128), F32),
            pltpu.VMEM((2 * REP, 1, 128), F32),
            pltpu.VMEM((2 * REP, CHUNK, COLS), BF16),
            pltpu.VMEM((2 * REP, CHUNK, COLS), BF16),
            pltpu.VMEM((2, 8, CHUNK, WIDE), F32),
            pltpu.VMEM((2, REP, SLOTS, WIDE), BF16),
            pltpu.VMEM((2, 3, SLOTS, WIDE), BF16),
            pltpu.VMEM((2, SLOTS, WIDE), BF16),
            pltpu.VMEM((2, 3, SLOTS, WIDE), BF16),
            pltpu.VMEM((2, 4, FOLD, WIDE), BF16),
            pltpu.VMEM((2, 3, FOLD, WIDE), BF16),
            pltpu.VMEM((FEAT, COLS), BF16),
            pltpu.SemaphoreType.DMA((MESSAGES,)),
            pltpu.SemaphoreType.DMA((MESSAGES,)),
            pltpu.SemaphoreType.DMA((6,)),
            pltpu.SemaphoreType.DMA((5,)),
        ],
        compiler_params=pltpu.CompilerParams(
            collective_id=0, has_side_effects=True, vmem_limit_bytes=limit
        ),
        cost_estimate=pl.CostEstimate(
            flops=6 * 256 * FEAT * COLS, bytes_accessed=4 * FEAT * COLS, transcendentals=64 * COLS
        ),
    )(counts, seq_cotangent, positions, targets, hidden, head_weight)
    return pl.pallas_call(
        hand_over,
        out_shape=shapes,
        in_specs=[hbm] * 3,
        out_specs=(hbm,) * 3,
        scratch_shapes=[
            pltpu.VMEM((FEAT, COLS), BF16),
            pltpu.VMEM((1, TOK, FEAT), BF16),
            pltpu.SMEM((REP,), F32),
            pltpu.SemaphoreType.DMA((6,)),
            pltpu.SemaphoreType.DMA((6,)),
        ],
        compiler_params=pltpu.CompilerParams(vmem_limit_bytes=limit),
    )(*results)


def solution(mesh):
    return jax.shard_map(
        shards,
        mesh=mesh,
        in_specs=(P("rep", "seq", "vocab"), P("vocab", ("seq", "rep")), P(), P(), P(), P()),
        out_specs=(P("vocab", ("seq", "rep")), P("rep", "seq", "vocab"), P()),
        check_vma=False,
    )
```

time: 728 us -> 78.6 us (0.11)
  the two profiles are of different devices: /device:TPU:2 before, /device:TPU:1 now
where the time goes in v1:
time: 78.6 us; the launch traced here: 77.7 us
  Pallas kernels  77.1 us (98%)
    pallas_call x1, Pallas kernels, shards(): pl.pallas_call(kernel, out_shape=shapes, in_specs=[hbm] * 6, out_specs=(h...  74.9 us
    pallas_call x1, Pallas kernels, shards(): pl.pallas_call(hand_over, out_shape=shapes, in_specs=[hbm] * 3, out_specs...  2.16 us

profile of v1, /device:TPU:1, one launch (start us, length us, event | category | flops | bytes accessed | tf_op | source)
XLA Modules:
  0.0 77.7 jit_solution(6714949092241329105)
XLA Ops:
  0.6 74.9 %shard_map.85 = (bf16[512,1280]{1,0:T(8,128)(2,1)}, bf16[1,64,512]{2,1,0:T(8,128)(2,1)}, f32[4]{0:T(128)}) custom-call(s32[4]{0:T(128)} %counts_hbm.1, f32[4]{0:T(128)} %cot_hbm.1, s32[4,64]{1,0:T(4,128)} %positions_hbm.1, s32[4,64]{1,0:T(4,128)} %targets_hbm.1, bf16[1,64,512]{2,1,0:T(8,128)(2,1)} %hidden_hbm.1, bf16[512,1280]{1,0:T(8,128)(2,1)} %weight_hbm.1), custom_call_target="tpu_custom_call" | custom-call | flops 1006632960 | bytes 2621440 | tf_op jit(solution)/shard_map/pallas_call | solution.py:489
  75.5 2.2 %shard_map.86 = (bf16[512,1280]{1,0:T(8,128)(2,1)}, bf16[1,64,512]{2,1,0:T(8,128)(2,1)}, f32[4]{0:T(128)}) custom-call(bf16[512,1280]{1,0:T(8,128)(2,1)} %get-tuple-element.6.head_in, bf16[1,64,512]{2,1,0:T(8,128)(2,1)} %get-tuple-element.7.hidden_in, f32[4]{0:T(128)} %get-tuple-element.8.losses_in), custom_call_target="tpu_custom_call" | custom-call | tf_op jit(solution)/shard_map/pallas_call | solution.py:541

commit v2 on v1

--- a/solution.py
+++ b/solution.py
@@ -19,21 +19,22 @@
 CHUNK = 32
 HALF = 16
 WIDE = FEAT // 2
+SPAN = COLS // 2
 
 PICK_CLASS = 0
 PICK_NEAR = 6
 PICK_REP = 14
 LOGIT_CORE = 20
-LOGIT_Y = 24
-STAT_SEQ = 30
-STAT_REP = 45
-GRAD_Y = 48
-GRAD_CORE = 54
-SCALE = 58
-ROW_REP = 65
-ROW_NEAR = 71
-ROW_CLASS = 79
-MESSAGES = 85
+LOGIT_Y = 28
+STAT_SEQ = 40
+STAT_REP = 55
+GRAD_Y = 58
+GRAD_CORE = 64
+SCALE = 68
+ROW_REP = 75
+ROW_NEAR = 81
+ROW_CLASS = 89
+MESSAGES = 95
 
 
 def iota(shape, dim):
@@ -245,51 +246,71 @@
             for d in (1, 2, 3)
         ])
 
-    def partial_logits(h, core):
+    def partial_logits(h, core, k):
         rows = picked[h, pl.ds(2 * core, 2)].reshape(2 * SLOTS, WIDE)
         return jnp.dot(
-            rows, weight[h * WIDE : (h + 1) * WIDE], preferred_element_type=F32
-        ).reshape(4, CHUNK, COLS)
+            rows, weight[h * WIDE : (h + 1) * WIDE, k * SPAN : (k + 1) * SPAN],
+            preferred_element_type=F32,
+        ).reshape(4, CHUNK, SPAN)
 
     for copy in rep_copies[0]:
         copy.wait_recv()
-    core_out[...] = partial_logits(0, 1 - c)
-    part[...] = partial_logits(0, c)
+    for k in range(2):
+        core_out[k] = partial_logits(0, 1 - c, k)
+        part[k] = partial_logits(0, c, k)
     for copy in rep_copies[1]:
         copy.wait_recv()
-    core_out[...] = core_out[...] + partial_logits(1, 1 - c)
     order = (2, 1, 3, 0)
-    core_copies = [
-        send(LOGIT_CORE + i, core_out.at[y_plus(s)], core_in.at[y_plus(s)], sibling)
-        for i, s in enumerate(order)
-    ]
-    part[...] = part[...] + partial_logits(1, c)
+    core_copies = []
+    for k in range(2):
+        core_out[k] = core_out[k] + partial_logits(1, 1 - c, k)
+        core_copies.append({
+            s: send(
+                LOGIT_CORE + 4 * k + s, core_out.at[k, y_plus(s)], core_in.at[k, y_plus(s)], sibling
+            )
+            for s in order
+        })
+    for k in range(2):
+        part[k] = part[k] + partial_logits(1, c, k)
 
     low, high = pl.ds(0, HALF), pl.ds(HALF, HALF)
-    y_copies = []
-    for i, s in enumerate(order):
-        core_copies[i].wait_recv()
-        at = y_plus(s)
-        part[at] = part[at] + core_in[at]
-        if s == 2:
-            y_copies.append(send(LOGIT_Y, part.at[at, low], y_fwd.at[0], at_y(1)))
-            y_copies.append(send(LOGIT_Y + 1, part.at[at, high], y_fwd.at[1], at_y(3)))
-        if s == 1:
-            y_copies.append(send(LOGIT_Y + 2, part.at[at, high], y_direct.at[1], at_y(1)))
-        if s == 3:
-            y_copies.append(send(LOGIT_Y + 3, part.at[at, low], y_direct.at[0], at_y(3)))
+    fwd_copies = []
+    last_copies = []
+    for s in order:
+        for k in range(2):
+            core_copies[k][s].wait_recv()
+            at = y_plus(s)
+            part[k, at] = part[k, at] + core_in[k, at]
+            number = LOGIT_Y + 6 * k
+            if s == 2:
+                fwd_copies.append((
+                    send(number, part.at[k, at, low], y_fwd.at[k, 0], at_y(1)),
+                    send(number + 1, part.at[k, at, high], y_fwd.at[k, 1], at_y(3)),
+                ))
+            if s == 1:
+                last_copies.append(
+                    send(number + 2, part.at[k, at, high], y_direct.at[k, 1], at_y(1))
+                )
+            if s == 3:
+                last_copies.append(
+                    send(number + 3, part.at[k, at, low], y_direct.at[k, 0], at_y(3))
+                )
+    for k in range(2):
+        number = LOGIT_Y + 6 * k
+        fwd_copies[k][0].wait_recv()
+        y_sum[k, 0] = y_fwd[k, 0] + part[k, y_plus(1), 0:HALF]
+        last_copies.append(send(number + 4, y_sum.at[k, 0], y_acc.at[k, 0], at_y(1)))
+        fwd_copies[k][1].wait_recv()
+        y_sum[k, 1] = y_fwd[k, 1] + part[k, y_plus(3), HALF:CHUNK]
+        last_copies.append(send(number + 5, y_sum.at[k, 1], y_acc.at[k, 1], at_y(3)))
     for h in range(2):
         picked_t[h * WIDE : (h + 1) * WIDE] = picked[h].reshape(REP * SLOTS, WIDE).T
-    y_copies[0].wait_recv()
-    y_sum[0] = y_fwd[0] + part[y_plus(1), 0:HALF]
-    y_copies.append(send(LOGIT_Y + 4, y_sum.at[0], y_acc.at[0], at_y(1)))
-    y_copies[1].wait_recv()
-    y_sum[1] = y_fwd[1] + part[y_plus(3), HALF:CHUNK]
-    y_copies.append(send(LOGIT_Y + 5, y_sum.at[1], y_acc.at[1], at_y(3)))
-    for copy in y_copies[2:]:
-        copy.wait_recv()
-    logits_ref[0:HALF] = part[y, 0:HALF] + (y_direct[0] + y_acc[0])
-    logits_ref[HALF:CHUNK] = part[y, HALF:CHUNK] + (y_direct[1] + y_acc[1])
+    for copy in last_copies:
+        copy.wait_recv()
+    for k in range(2):
+        columns = pl.ds(k * SPAN, SPAN)
+        logits_ref[0:HALF, columns] = part[k, y, 0:HALF] + (y_direct[k, 0] + y_acc[k, 0])
+        logits_ref[HALF:CHUNK, columns] = part[k, y, HALF:CHUNK] + (y_direct[k, 1] + y_acc[k, 1])
 
     loads[3].wait()
     my_seq = 2 * c + lax.div(y, 2)
@@ -435,8 +456,12 @@
             for d in (1, 2, 3)
         ])
     head_copies += [head_part(3), head_part(4)]
+    for copy in started[: -2 * 3]:
+        copy.wait_send()
     for q in range(REP):
         losses_ref[q] = jnp.sum(between(scales[2 * q] + scales[2 * q + 1], 2 * CHUNK))
+    for copy in head_copies:
+        copy.wait()
     put = jnp.where(put_at, 1.0, 0.0).astype(BF16)
     for h in range(2):
         for copy in class_copies[h]:
@@ -450,10 +475,9 @@
             put, final, preferred_element_type=F32
         ).astype(BF16)
 
-    for copy in started:
-        copy.wait_send()
-    for copy in head_copies:
-        copy.wait()
+    for copies in class_copies:
+        for copy in copies:
+            copy.wait_send()
 
 
 def hand_over(
@@ -505,13 +529,13 @@
             pltpu.VMEM((FEAT, REP * SLOTS), BF16),
             pltpu.VMEM((8, CHUNK, 1), jnp.int32),
             pltpu.VMEM((2, 8, CHUNK, WIDE), F32),
-            pltpu.VMEM((4, CHUNK, COLS), F32),
-            pltpu.VMEM((4, CHUNK, COLS), F32),
-            pltpu.VMEM((4, CHUNK, COLS), F32),
-            pltpu.VMEM((2, HALF, COLS), F32),
-            pltpu.VMEM((2, HALF, COLS), F32),
-            pltpu.VMEM((2, HALF, COLS), F32),
-            pltpu.VMEM((2, HALF, COLS), F32),
+            pltpu.VMEM((2, 4, CHUNK, SPAN), F32),
+            pltpu.VMEM((2, 4, CHUNK, SPAN), F32),
+            pltpu.VMEM((2, 4, CHUNK, SPAN), F32),
+            pltpu.VMEM((2, 2, HALF, SPAN), F32),
+            pltpu.VMEM((2, 2, HALF, SPAN), F32),
+            pltpu.VMEM((2, 2, HALF, SPAN), F32),
+            pltpu.VMEM((2, 2, HALF, SPAN), F32),
             pltpu.VMEM((CHUNK, COLS), F32),
             pltpu.VMEM((SEQ, 1, 128), F32),
             pltpu.VMEM((REP, 1, 128), F32),

time: 78.6 us -> 77.9 us (level)
  no operation moved by 1% of the time
where the time goes in v2:
time: 77.9 us; the launch traced here: 77 us
  Pallas kernels  76.4 us (98%)
    pallas_call x1, Pallas kernels, shards(): pl.pallas_call(kernel, out_shape=shapes, in_specs=[hbm] * 6, out_specs=(h...  74.2 us
    pallas_call x1, Pallas kernels, shards(): pl.pallas_call(hand_over, out_shape=shapes, in_specs=[hbm] * 3, out_specs...  2.16 us

profile of v2, /device:TPU:1, one launch (start us, length us, event | category | flops | bytes accessed | tf_op | source)
XLA Modules:
  0.0 77.0 jit_solution(2556753344272663770)
XLA Ops:
  0.6 74.2 %shard_map.85 = (bf16[512,1280]{1,0:T(8,128)(2,1)}, bf16[1,64,512]{2,1,0:T(8,128)(2,1)}, f32[4]{0:T(128)}) custom-call(s32[4]{0:T(128)} %counts_hbm.1, f32[4]{0:T(128)} %cot_hbm.1, s32[4,64]{1,0:T(4,128)} %positions_hbm.1, s32[4,64]{1,0:T(4,128)} %targets_hbm.1, bf16[1,64,512]{2,1,0:T(8,128)(2,1)} %hidden_hbm.1, bf16[512,1280]{1,0:T(8,128)(2,1)} %weight_hbm.1), custom_call_target="tpu_custom_call" | custom-call | flops 1006632960 | bytes 2621440 | tf_op jit(solution)/shard_map/pallas_call | solution.py:513
  74.9 2.2 %shard_map.86 = (bf16[512,1280]{1,0:T(8,128)(2,1)}, bf16[1,64,512]{2,1,0:T(8,128)(2,1)}, f32[4]{0:T(128)}) custom-call(bf16[512,1280]{1,0:T(8,128)(2,1)} %get-tuple-element.6.head_in, bf16[1,64,512]{2,1,0:T(8,128)(2,1)} %get-tuple-element.7.hidden_in, f32[4]{0:T(128)} %get-tuple-element.8.losses_in), custom_call_target="tpu_custom_call" | custom-call | tf_op jit(solution)/shard_map/pallas_call | solution.py:565

commit v3 on v2

--- a/solution.py
+++ b/solution.py
@@ -34,7 +34,8 @@
 ROW_REP = 75
 ROW_NEAR = 81
 ROW_CLASS = 89
-MESSAGES = 95
+TARGET_REP = 95
+MESSAGES = 98
 
 
 def iota(shape, dim):
@@ -94,7 +95,8 @@
 def kernel(
     counts_hbm, cot_hbm, positions_hbm, targets_hbm, hidden_hbm, weight_hbm,
     head_hbm, grad_ref, losses_ref,
-    counts_ref, cot_ref, positions_ref, targets_ref, hidden_ref, weight, pick_class, pick_own, pick_near, picked, picked_t, target_cols, target_rows,
+    counts_ref, cot_ref, positions_ref, targets_ref, hidden_ref,
+    weight, pick_class, pick_own, pick_near, picked, picked_t, target_cols, target_out, target_in,
     core_out, core_in, part, y_fwd, y_sum, y_direct, y_acc, logits_ref,
     stat_seq, stat_rep, scales, exps, grads,
     row_sums, row_out, row_in, near_out, near_in, class_out, class_in, head_out,
@@ -212,10 +214,12 @@
 
     def head_at_targets(h):
         hot = [jnp.where(column == target_cols[i], 1.0, 0.0).astype(BF16) for i in range(8)]
-        target_rows[h] = lax.dot_general(
+        there = lax.dot_general(
             jnp.concatenate(hot, axis=0), weight[h * WIDE : (h + 1) * WIDE],
             (((1,), (1,)), ((), ())), preferred_element_type=F32,
-        ).reshape(8, CHUNK, WIDE)
+        ).reshape(REP, SLOTS, WIDE)
+        for q in range(REP):
+            target_out[q, h] = there[q].astype(BF16)
 
     loads[5].wait()
     head_at_targets(0)
@@ -272,6 +276,12 @@
         })
     for k in range(2):
         part[k] = part[k] + partial_logits(1, c, k)
+    target_copies = [
+        send(
+            TARGET_REP + d - 1, target_out.at[lax.rem(x + d, REP)], target_in.at[d - 1], at_x(d)
+        )
+        for d in (1, 2, 3)
+    ]
 
     low, high = pl.ds(0, HALF), pl.ds(HALF, HALF)
     fwd_copies = []
@@ -338,7 +348,8 @@
     max_row = to_row(local_max, 0)
     stat_seq[z] = max_row + to_row(local_sum, CHUNK) + to_row(local_target, 2 * CHUNK)
     seq_copies = [
-        send(STAT_SEQ + d - 1, stat_seq.at[z], stat_seq.at[z], at_z(d)) for d in range(1, SEQ)
+        send(STAT_SEQ + d - 1, stat_seq.at[z], stat_seq.at[z], at_z(d))
+        for d in (8, 7, 9, 6, 10, 5, 11, 4, 12, 3, 13, 2, 14, 1, 15)
     ]
 
     up_low.wait_recv()
@@ -350,68 +361,93 @@
     down_low.wait_recv()
     core_copies.append(send(GRAD_CORE + 2, after, after, sibling))
 
-    for copy in seq_copies:
-        copy.wait_recv()
-    stat_rep[x] = pack_stats(*merge_stats(stat_seq, SEQ))
-    copies = [send(STAT_REP + d - 1, stat_rep.at[x], stat_rep.at[x], at_x(d)) for d in (1, 2, 3)]
     up_again.wait_recv()
     down_again.wait_recv()
     across = exps.at[4 * c + y_plus(2)]
     core_copies.append(send(GRAD_CORE + 3, across, across, sibling))
-    for copy in copies:
-        copy.wait_recv()
-    total_max, total_sum, target_logit = merge_stats(stat_rep, REP)
-
-    lane = iota((1, 128), 1)
-    live = (lane < CHUNK) & (lane + first_slot < my_count)
-    count_row = jnp.full((1, 128), my_count.astype(F32), F32)
-    weight_row = jnp.where(live, jnp.full((1, 128), my_cot, F32) / count_row, 0.0)
-    factor = jnp.where(live, weight_row * (jnp.exp(max_row - total_max) / total_sum), 0.0)
-    at_target = jnp.where(
-        live, weight_row * (jnp.exp(target_logit - total_max) / total_sum - 1.0), 0.0
-    )
-    row_loss = jnp.where(live, (jnp.log(total_sum) + total_max - target_logit) / count_row, 0.0)
-    scales[my_chunk] = pack_stats(factor, at_target, row_loss)
-    scale_copies = [
-        send(SCALE + d - 1, scales.at[my_chunk], scales.at[my_chunk], {"vocab": lax.rem(v + d, 8)})
-        for d in range(1, 8)
+
+    for copy in seq_copies:
+        copy.wait_recv()
+    stat_rep[x] = pack_stats(*merge_stats(stat_seq, SEQ)) + to_row(local_max, 3 * CHUNK)
+    stat_copies = [
+        send(STAT_REP + d - 1, stat_rep.at[x], stat_rep.at[x], at_x(d)) for d in (1, 2, 3)
     ]
 
     def head_times(core):
         block = exps[pl.ds(4 * core, 4)].reshape(4 * CHUNK, COLS)
         for h in range(2):
-            row_sums[h, pl.ds(4 * core, 4)] = lax.dot_general(
+            rows = lax.dot_general(
                 block, weight[h * WIDE : (h + 1) * WIDE], (((1,), (1,)), ((), ())),
                 preferred_element_type=F32,
-            ).reshape(4, CHUNK, WIDE)
+            ).reshape(2, SLOTS, WIDE)
+            row_sums[h, pl.ds(2 * core, 2)] = rows
+            row_out[h, pl.ds(2 * core, 2)] = rows.astype(BF16)
 
     head_times(c)
     for copy in core_copies:
         copy.wait_recv()
     head_times(1 - c)
-    for copy in scale_copies:
-        copy.wait_recv()
-    factors = [to_column(scales[i], CHUNK) for i in range(8)]
-    at_targets = [
-        to_column(scales[i], CHUNK, CHUNK).astype(BF16).astype(F32) for i in range(8)
-    ]
-    rep_copies = []
-    for h in range(2):
-        for i in range(8):
-            rows = factors[i] * row_sums[h, i] + at_targets[i] * target_rows[h, i]
-            row_sums[h, i] = rows
-            row_out[h, i // 2, CHUNK * (i % 2) : CHUNK * (i % 2 + 1)] = rows.astype(BF16)
-        rep_copies.append([
+    rep_copies = [
+        [
             send(
                 ROW_REP + 3 * h + d - 1, row_out.at[h, lax.rem(x + d, REP)], row_in.at[h, d - 1],
                 at_x(d),
             )
             for d in (1, 2, 3)
-        ])
-    for i in range(8):
-        values = exps[i].astype(F32) * factors[i]
-        grads[i] = jnp.where(column == target_cols[i], at_targets[i], values).astype(BF16)
-    owns = [row_sums[h, pl.ds(2 * x, 2)].reshape(SLOTS, WIDE) for h in range(2)]
+        ]
+        for h in range(2)
+    ]
+
+    for copy in stat_copies:
+        copy.wait_recv()
+    total_max, total_sum, target_logit = merge_stats(stat_rep, REP)
+    lane = iota((1, 128), 1)
+    live = (lane < CHUNK) & (lane + first_slot < my_count)
+    count_row = jnp.full((1, 128), my_count.astype(F32), F32)
+    weight_row = jnp.where(live, jnp.full((1, 128), my_cot, F32) / count_row, 0.0)
+    factor_row = jnp.zeros((1, 128), F32)
+    for i in range(REP):
+        there = jnp.exp(turn(stat_rep[i], 3 * CHUNK) - total_max) / total_sum
+        factor = jnp.where(live, weight_row * there, 0.0)
+        factor_row = factor_row + (turn(factor, 128 - i * CHUNK) if i else factor)
+    at_target = jnp.where(
+        live, weight_row * (jnp.exp(target_logit - total_max) / total_sum - 1.0), 0.0
+    )
+    row_loss = jnp.where(live, (jnp.log(total_sum) + total_max - target_logit) / count_row, 0.0)
+    scales[my_chunk, 0:1] = factor_row
+    scales[my_chunk, 1:2] = at_target + turn(row_loss, 128 - CHUNK)
+    scale_copies = [
+        send(SCALE + d - 1, scales.at[my_chunk], scales.at[my_chunk], {"vocab": lax.rem(v + d, 8)})
+        for d in range(1, 8)
+    ]
+    for copy in scale_copies:
+        copy.wait_recv()
+
+    def slots_of_mine(part_of, first):
+        return jnp.concatenate(
+            [to_column(scales[2 * x + i, part_of : part_of + 1], CHUNK, first) for i in range(2)],
+            axis=0,
+        )
+
+    slot_factors = [
+        slots_of_mine(0, CHUNK * lax.rem(x + REP - d, REP)) for d in range(REP)
+    ]
+    slot_target = slots_of_mine(1, 0).astype(BF16).astype(F32)
+    for copy in target_copies:
+        copy.wait_recv()
+    owns = []
+    for h in range(2):
+        column_sum = target_out[x, h].astype(F32)
+        for i in range(3):
+            column_sum = column_sum + target_in[i, h].astype(F32)
+        owns.append(slot_target * column_sum + slot_factors[0] * row_sums[h, x])
+
+    def scale_grads():
+        for i in range(8):
+            factor = to_column(scales[i, 0:1], CHUNK, CHUNK * x)
+            at_own = to_column(scales[i, 1:2], CHUNK)
+            values = exps[i].astype(F32) * factor
+            grads[i] = jnp.where(column == target_cols[i], at_own, values).astype(BF16)
 
     def head_part(i):
         columns = pl.ds(i * 256, 256)
@@ -430,10 +466,11 @@
         for copy in rep_copies[h]:
             copy.wait_recv()
         for i in range(3):
-            owns[h] = owns[h] + row_in[h, i].astype(F32)
+            owns[h] = owns[h] + slot_factors[i + 1] * row_in[h, i].astype(F32)
         near_out[h] = owns[h].astype(BF16)
         near_copies.append(send_near(ROW_NEAR + 4 * h, near_out.at[h], near_in.at[h]))
-    head_copies = [head_part(0), head_part(1), head_part(2)]
+    scale_grads()
+    head_copies = [head_part(0), head_part(1)]
     mine_rows = []
     class_copies = []
     for h in range(2):
@@ -455,11 +492,11 @@
             )
             for d in (1, 2, 3)
         ])
-    head_copies += [head_part(3), head_part(4)]
+    head_copies += [head_part(2), head_part(3), head_part(4)]
     for copy in started[: -2 * 3]:
         copy.wait_send()
     for q in range(REP):
-        losses_ref[q] = jnp.sum(between(scales[2 * q] + scales[2 * q + 1], 2 * CHUNK))
+        losses_ref[q] = jnp.sum(between(scales[2 * q, 1:2] + scales[2 * q + 1, 1:2], CHUNK))
     for copy in head_copies:
         copy.wait()
     put = jnp.where(put_at, 1.0, 0.0).astype(BF16)
@@ -528,7 +565,8 @@
             pltpu.VMEM((2, REP, SLOTS, WIDE), BF16),
             pltpu.VMEM((FEAT, REP * SLOTS), BF16),
             pltpu.VMEM((8, CHUNK, 1), jnp.int32),
-            pltpu.VMEM((2, 8, CHUNK, WIDE), F32),
+            pltpu.VMEM((REP, 2, SLOTS, WIDE), BF16),
+            pltpu.VMEM((3, 2, SLOTS, WIDE), BF16),
             pltpu.VMEM((2, 4, CHUNK, SPAN), F32),
             pltpu.VMEM((2, 4, CHUNK, SPAN), F32),
             pltpu.VMEM((2, 4, CHUNK, SPAN), F32),
@@ -539,10 +577,10 @@
             pltpu.VMEM((CHUNK, COLS), F32),
             pltpu.VMEM((SEQ, 1, 128), F32),
             pltpu.VMEM((REP, 1, 128), F32),
-            pltpu.VMEM((2 * REP, 1, 128), F32),
+            pltpu.VMEM((2 * REP, 2, 128), F32),
             pltpu.VMEM((2 * REP, CHUNK, COLS), BF16),
             pltpu.VMEM((2 * REP, CHUNK, COLS), BF16),
-            pltpu.VMEM((2, 8, CHUNK, WIDE), F32),
+            pltpu.VMEM((2, REP, SLOTS, WIDE), F32),
             pltpu.VMEM((2, REP, SLOTS, WIDE), BF16),
             pltpu.VMEM((2, 3, SLOTS, WIDE), BF16),
             pltpu.VMEM((2, SLOTS, WIDE), BF16),

time: 77.9 us -> 76 us (0.976)
  Pallas kernels: 76.4 us -> 75.2 us
    pallas_call x1, Pallas kernels: 74.2 us -> 73 us  [shards(): pl.pallas_call(kernel, out_shape=shapes, in_specs=[hbm] * 6, out_specs=(h...]
where the time goes in v3:
time: 76 us; the launch traced here: 75.8 us
  Pallas kernels  75.2 us (99%)
    pallas_call x1, Pallas kernels, shards(): pl.pallas_call(kernel, out_shape=shapes, in_specs=[hbm] * 6, out_specs=(h...  73 us
    pallas_call x1, Pallas kernels, shards(): pl.pallas_call(hand_over, out_shape=shapes, in_specs=[hbm] * 3, out_specs...  2.16 us

profile of v3, /device:TPU:1, one launch (start us, length us, event | category | flops | bytes accessed | tf_op | source)
XLA Modules:
  0.0 75.8 jit_solution(6772116145474668388)
XLA Ops:
  0.6 73.0 %shard_map.85 = (bf16[512,1280]{1,0:T(8,128)(2,1)}, bf16[1,64,512]{2,1,0:T(8,128)(2,1)}, f32[4]{0:T(128)}) custom-call(s32[4]{0:T(128)} %counts_hbm.1, f32[4]{0:T(128)} %cot_hbm.1, s32[4,64]{1,0:T(4,128)} %positions_hbm.1, s32[4,64]{1,0:T(4,128)} %targets_hbm.1, bf16[1,64,512]{2,1,0:T(8,128)(2,1)} %hidden_hbm.1, bf16[512,1280]{1,0:T(8,128)(2,1)} %weight_hbm.1), custom_call_target="tpu_custom_call" | custom-call | flops 1006632960 | bytes 2621440 | tf_op jit(solution)/shard_map/pallas_call | solution.py:550
  73.7 2.2 %shard_map.86 = (bf16[512,1280]{1,0:T(8,128)(2,1)}, bf16[1,64,512]{2,1,0:T(8,128)(2,1)}, f32[4]{0:T(128)}) custom-call(bf16[512,1280]{1,0:T(8,128)(2,1)} %get-tuple-element.6.head_in, bf16[1,64,512]{2,1,0:T(8,128)(2,1)} %get-tuple-element.7.hidden_in, f32[4]{0:T(128)} %get-tuple-element.8.losses_in), custom_call_target="tpu_custom_call" | custom-call | tf_op jit(solution)/shard_map/pallas_call | solution.py:603

commit v4 on v3

--- a/solution.py
+++ b/solution.py
@@ -29,13 +29,13 @@
 STAT_SEQ = 40
 STAT_REP = 55
 GRAD_Y = 58
-GRAD_CORE = 64
-SCALE = 68
-ROW_REP = 75
-ROW_NEAR = 81
-ROW_CLASS = 89
-TARGET_REP = 95
-MESSAGES = 98
+GRAD_CORE = 66
+SCALE = 69
+ROW_REP = 76
+ROW_NEAR = 82
+ROW_CLASS = 90
+TARGET_REP = 96
+MESSAGES = 99
 
 
 def iota(shape, dim):
@@ -122,6 +122,9 @@
     def at_y(shift):
         return {"vocab": y_plus(shift) * 2 + c}
 
+    def across_y(shift):
+        return {"vocab": y_plus(shift) * 2 + 1 - c}
+
     def load(number, src, dst):
         copy = pltpu.make_async_copy(src, dst, load_sem.at[number])
         copy.start()
@@ -190,7 +193,7 @@
                 PICK_CLASS + 3 * h + d - 1, pick_class.at[h, member], pick_class.at[h, member],
                 at_z(4 * d),
             )
-            for d in (1, 2, 3)
+            for d in (2, 1, 3)
         ]
         for h in range(2)
     ]
@@ -353,45 +356,47 @@
     ]
 
     up_low.wait_recv()
-    up_again = send(GRAD_Y + 4, before.at[low], before.at[low], at_y(1))
+    relays = [
+        send(GRAD_Y + 4, before.at[low], before.at[low], at_y(1)),
+        send(GRAD_Y + 5, before.at[low], before.at[low], across_y(1)),
+    ]
     down_high.wait_recv()
-    down_again = send(GRAD_Y + 5, after.at[high], after.at[high], at_y(3))
+    relays.append(send(GRAD_Y + 6, after.at[high], after.at[high], at_y(3)))
+    relays.append(send(GRAD_Y + 7, after.at[high], after.at[high], across_y(3)))
     up_high.wait_recv()
     core_copies.append(send(GRAD_CORE + 1, before, before, sibling))
     down_low.wait_recv()
     core_copies.append(send(GRAD_CORE + 2, after, after, sibling))
 
-    up_again.wait_recv()
-    down_again.wait_recv()
-    across = exps.at[4 * c + y_plus(2)]
-    core_copies.append(send(GRAD_CORE + 3, across, across, sibling))
-
-    for copy in seq_copies:
-        copy.wait_recv()
-    stat_rep[x] = pack_stats(*merge_stats(stat_seq, SEQ)) + to_row(local_max, 3 * CHUNK)
-    stat_copies = [
-        send(STAT_REP + d - 1, stat_rep.at[x], stat_rep.at[x], at_x(d)) for d in (1, 2, 3)
-    ]
-
-    def head_times(core):
-        block = exps[pl.ds(4 * core, 4)].reshape(4 * CHUNK, COLS)
+    def head_times(chunks):
+        block = jnp.concatenate([exps[i] for i in chunks], axis=0)
         for h in range(2):
             rows = lax.dot_general(
                 block, weight[h * WIDE : (h + 1) * WIDE], (((1,), (1,)), ((), ())),
                 preferred_element_type=F32,
-            ).reshape(2, SLOTS, WIDE)
-            row_sums[h, pl.ds(2 * core, 2)] = rows
-            row_out[h, pl.ds(2 * core, 2)] = rows.astype(BF16)
-
-    head_times(c)
+            )
+            for n, i in enumerate(chunks):
+                row_sums[h, i] = rows[n * CHUNK : (n + 1) * CHUNK]
+                row_out[h, i] = rows[n * CHUNK : (n + 1) * CHUNK].astype(BF16)
+
+    head_times([4 * c + y_plus(i) for i in (0, 1, 3)])
+    for copy in seq_copies:
+        copy.wait_recv()
+    stat_rep[x] = pack_stats(*merge_stats(stat_seq, SEQ)) + to_row(local_max, 3 * CHUNK)
+    stat_copies = [
+        send(STAT_REP + d - 1, stat_rep.at[x], stat_rep.at[x], at_x(d)) for d in (1, 2, 3)
+    ]
     for copy in core_copies:
         copy.wait_recv()
-    head_times(1 - c)
+    head_times([4 * (1 - c) + y_plus(i) for i in (0, 1, 3)])
+    for copy in relays:
+        copy.wait_recv()
+    head_times([4 * c + y_plus(2), 4 * (1 - c) + y_plus(2)])
     rep_copies = [
         [
             send(
-                ROW_REP + 3 * h + d - 1, row_out.at[h, lax.rem(x + d, REP)], row_in.at[h, d - 1],
-                at_x(d),
+                ROW_REP + 3 * h + d - 1, row_out.at[h, pl.ds(2 * lax.rem(x + d, REP), 2)],
+                row_in.at[h, d - 1], at_x(d),
             )
             for d in (1, 2, 3)
         ]
@@ -440,7 +445,7 @@
         column_sum = target_out[x, h].astype(F32)
         for i in range(3):
             column_sum = column_sum + target_in[i, h].astype(F32)
-        owns.append(slot_target * column_sum + slot_factors[0] * row_sums[h, x])
+        owns.append(slot_target * column_sum + slot_factors[0] * row_sums[h, pl.ds(2 * x, 2)].reshape(SLOTS, WIDE))
 
     def scale_grads():
         for i in range(8):
@@ -466,7 +471,7 @@
         for copy in rep_copies[h]:
             copy.wait_recv()
         for i in range(3):
-            owns[h] = owns[h] + slot_factors[i + 1] * row_in[h, i].astype(F32)
+            owns[h] = owns[h] + slot_factors[i + 1] * row_in[h, i].reshape(SLOTS, WIDE).astype(F32)
         near_out[h] = owns[h].astype(BF16)
         near_copies.append(send_near(ROW_NEAR + 4 * h, near_out.at[h], near_in.at[h]))
     scale_grads()
@@ -490,7 +495,7 @@
                 ROW_CLASS + 3 * h + d - 1, class_out.at[h, lax.rem(member + d, 4)],
                 class_in.at[h, d - 1], at_z(4 * d),
             )
-            for d in (1, 2, 3)
+            for d in (2, 1, 3)
         ])
     head_copies += [head_part(2), head_part(3), head_part(4)]
     for copy in started[: -2 * 3]:
@@ -580,9 +585,9 @@
             pltpu.VMEM((2 * REP, 2, 128), F32),
             pltpu.VMEM((2 * REP, CHUNK, COLS), BF16),
             pltpu.VMEM((2 * REP, CHUNK, COLS), BF16),
-            pltpu.VMEM((2, REP, SLOTS, WIDE), F32),
-            pltpu.VMEM((2, REP, SLOTS, WIDE), BF16),
-            pltpu.VMEM((2, 3, SLOTS, WIDE), BF16),
+            pltpu.VMEM((2, 2 * REP, CHUNK, WIDE), F32),
+            pltpu.VMEM((2, 2 * REP, CHUNK, WIDE), BF16),
+            pltpu.VMEM((2, 3, 2, CHUNK, WIDE), BF16),
             pltpu.VMEM((2, SLOTS, WIDE), BF16),
             pltpu.VMEM((2, 3, SLOTS, WIDE), BF16),
             pltpu.VMEM((2, 4, FOLD, WIDE), BF16),

time: 76 us -> 74.2 us (0.976)
  Pallas kernels: 75.2 us -> 73.4 us
    pallas_call x1, Pallas kernels: 73 us -> 71.3 us  [shards(): pl.pallas_call(kernel, out_shape=shapes, in_specs=[hbm] * 6, out_specs=(h...]
where the time goes in v4:
time: 74.2 us; the launch traced here: 74.1 us
  Pallas kernels  73.4 us (99%)
    pallas_call x1, Pallas kernels, shards(): pl.pallas_call(kernel, out_shape=shapes, in_specs=[hbm] * 6, out_specs=(h...  71.3 us
    pallas_call x1, Pallas kernels, shards(): pl.pallas_call(hand_over, out_shape=shapes, in_specs=[hbm] * 3, out_specs...  2.16 us

profile of v4, /device:TPU:1, one launch (start us, length us, event | category | flops | bytes accessed | tf_op | source)
XLA Modules:
  0.0 74.1 jit_solution(14706201608914727604)
XLA Ops:
  0.6 71.3 %shard_map.85 = (bf16[512,1280]{1,0:T(8,128)(2,1)}, bf16[1,64,512]{2,1,0:T(8,128)(2,1)}, f32[4]{0:T(128)}) custom-call(s32[4]{0:T(128)} %counts_hbm.1, f32[4]{0:T(128)} %cot_hbm.1, s32[4,64]{1,0:T(4,128)} %positions_hbm.1, s32[4,64]{1,0:T(4,128)} %targets_hbm.1, bf16[1,64,512]{2,1,0:T(8,128)(2,1)} %hidden_hbm.1, bf16[512,1280]{1,0:T(8,128)(2,1)} %weight_hbm.1), custom_call_target="tpu_custom_call" | custom-call | flops 1006632960 | bytes 2621440 | tf_op jit(solution)/shard_map/pallas_call | solution.py:555
  71.9 2.2 %shard_map.86 = (bf16[512,1280]{1,0:T(8,128)(2,1)}, bf16[1,64,512]{2,1,0:T(8,128)(2,1)}, f32[4]{0:T(128)}) custom-call(bf16[512,1280]{1,0:T(8,128)(2,1)} %get-tuple-element.6.head_in, bf16[1,64,512]{2,1,0:T(8,128)(2,1)} %get-tuple-element.7.hidden_in, f32[4]{0:T(128)} %get-tuple-element.8.losses_in), custom_call_target="tpu_custom_call" | custom-call | tf_op jit(solution)/shard_map/pallas_call | solution.py:608

commit v5 on v4

--- a/solution.py
+++ b/solution.py
@@ -201,10 +201,10 @@
     def send_near(number, src, dst):
         low, high = pl.ds(0, 32), pl.ds(32, 32)
         return [
+            send(number + 2, src.at[low], dst.at[2, low], at_z(2)),
+            send(number + 3, src.at[high], dst.at[2, high], at_z(-2)),
             send(number, src, dst.at[0], at_z(1)),
             send(number + 1, src, dst.at[1], at_z(-1)),
-            send(number + 2, src.at[low], dst.at[2, low], at_z(2)),
-            send(number + 3, src.at[high], dst.at[2, high], at_z(-2)),
         ]
 
     loads[4].wait()
@@ -250,7 +250,7 @@
         picked[h, x] = total.astype(BF16)
         rep_copies.append([
             send(PICK_REP + 3 * h + d - 1, picked.at[h, x], picked.at[h, x], at_x(d))
-            for d in (1, 2, 3)
+            for d in (2, 1, 3)
         ])
 
     def partial_logits(h, core, k):
@@ -368,18 +368,18 @@
     down_low.wait_recv()
     core_copies.append(send(GRAD_CORE + 2, after, after, sibling))
 
-    def head_times(chunks):
+    def head_times(h, chunks):
         block = jnp.concatenate([exps[i] for i in chunks], axis=0)
-        for h in range(2):
-            rows = lax.dot_general(
-                block, weight[h * WIDE : (h + 1) * WIDE], (((1,), (1,)), ((), ())),
-                preferred_element_type=F32,
-            )
-            for n, i in enumerate(chunks):
-                row_sums[h, i] = rows[n * CHUNK : (n + 1) * CHUNK]
-                row_out[h, i] = rows[n * CHUNK : (n + 1) * CHUNK].astype(BF16)
-
-    head_times([4 * c + y_plus(i) for i in (0, 1, 3)])
+        rows = lax.dot_general(
+            block, weight[h * WIDE : (h + 1) * WIDE], (((1,), (1,)), ((), ())),
+            preferred_element_type=F32,
+        )
+        for n, i in enumerate(chunks):
+            row_sums[h, i] = rows[n * CHUNK : (n + 1) * CHUNK]
+            row_out[h, i] = rows[n * CHUNK : (n + 1) * CHUNK].astype(BF16)
+
+    for h in range(2):
+        head_times(h, [4 * c + y_plus(i) for i in (0, 1, 3)])
     for copy in seq_copies:
         copy.wait_recv()
     stat_rep[x] = pack_stats(*merge_stats(stat_seq, SEQ)) + to_row(local_max, 3 * CHUNK)
@@ -388,20 +388,20 @@
     ]
     for copy in core_copies:
         copy.wait_recv()
-    head_times([4 * (1 - c) + y_plus(i) for i in (0, 1, 3)])
+    for h in range(2):
+        head_times(h, [4 * (1 - c) + y_plus(i) for i in (0, 1, 3)])
     for copy in relays:
         copy.wait_recv()
-    head_times([4 * c + y_plus(2), 4 * (1 - c) + y_plus(2)])
-    rep_copies = [
-        [
+    rep_copies = []
+    for h in range(2):
+        head_times(h, [4 * c + y_plus(2), 4 * (1 - c) + y_plus(2)])
+        rep_copies.append([
             send(
                 ROW_REP + 3 * h + d - 1, row_out.at[h, pl.ds(2 * lax.rem(x + d, REP), 2)],
                 row_in.at[h, d - 1], at_x(d),
             )
-            for d in (1, 2, 3)
-        ]
-        for h in range(2)
-    ]
+            for d in (2, 1, 3)
+        ])
 
     for copy in stat_copies:
         copy.wait_recv()

time: 74.2 us -> 73.6 us (level)
  no operation moved by 1% of the time
where the time goes in v5:
time: 73.6 us; the launch traced here: 73.5 us
  Pallas kernels  72.8 us (99%)
    pallas_call x1, Pallas kernels, shards(): pl.pallas_call(kernel, out_shape=shapes, in_specs=[hbm] * 6, out_specs=(h...  70.7 us
    pallas_call x1, Pallas kernels, shards(): pl.pallas_call(hand_over, out_shape=shapes, in_specs=[hbm] * 3, out_specs...  2.16 us

profile of v5, /device:TPU:1, one launch (start us, length us, event | category | flops | bytes accessed | tf_op | source)
XLA Modules:
  0.0 73.5 jit_solution(7316384750838273285)
XLA Ops:
  0.6 70.7 %shard_map.85 = (bf16[512,1280]{1,0:T(8,128)(2,1)}, bf16[1,64,512]{2,1,0:T(8,128)(2,1)}, f32[4]{0:T(128)}) custom-call(s32[4]{0:T(128)} %counts_hbm.1, f32[4]{0:T(128)} %cot_hbm.1, s32[4,64]{1,0:T(4,128)} %positions_hbm.1, s32[4,64]{1,0:T(4,128)} %targets_hbm.1, bf16[1,64,512]{2,1,0:T(8,128)(2,1)} %hidden_hbm.1, bf16[512,1280]{1,0:T(8,128)(2,1)} %weight_hbm.1), custom_call_target="tpu_custom_call" | custom-call | flops 1006632960 | bytes 2621440 | tf_op jit(solution)/shard_map/pallas_call | solution.py:555
  71.3 2.2 %shard_map.86 = (bf16[512,1280]{1,0:T(8,128)(2,1)}, bf16[1,64,512]{2,1,0:T(8,128)(2,1)}, f32[4]{0:T(128)}) custom-call(bf16[512,1280]{1,0:T(8,128)(2,1)} %get-tuple-element.6.head_in, bf16[1,64,512]{2,1,0:T(8,128)(2,1)} %get-tuple-element.7.hidden_in, f32[4]{0:T(128)} %get-tuple-element.8.losses_in), custom_call_target="tpu_custom_call" | custom-call | tf_op jit(solution)/shard_map/pallas_call | solution.py:608

commit v6 on v5

--- a/solution.py
+++ b/solution.py
@@ -252,6 +252,8 @@
             send(PICK_REP + 3 * h + d - 1, picked.at[h, x], picked.at[h, x], at_x(d))
             for d in (2, 1, 3)
         ])
+
+    gathered = len(started)
 
     def partial_logits(h, core, k):
         rows = picked[h, pl.ds(2 * core, 2)].reshape(2 * SLOTS, WIDE)
@@ -318,6 +320,8 @@
         last_copies.append(send(number + 5, y_sum.at[k, 1], y_acc.at[k, 1], at_y(3)))
     for h in range(2):
         picked_t[h * WIDE : (h + 1) * WIDE] = picked[h].reshape(REP * SLOTS, WIDE).T
+    for copy in started[:gathered]:
+        copy.wait_send()
     for copy in last_copies:
         copy.wait_recv()
     for k in range(2):
@@ -384,7 +388,7 @@
         copy.wait_recv()
     stat_rep[x] = pack_stats(*merge_stats(stat_seq, SEQ)) + to_row(local_max, 3 * CHUNK)
     stat_copies = [
-        send(STAT_REP + d - 1, stat_rep.at[x], stat_rep.at[x], at_x(d)) for d in (1, 2, 3)
+        send(STAT_REP + d - 1, stat_rep.at[x], stat_rep.at[x], at_x(d)) for d in (2, 1, 3)
     ]
     for copy in core_copies:
         copy.wait_recv()
@@ -475,7 +479,6 @@
         near_out[h] = owns[h].astype(BF16)
         near_copies.append(send_near(ROW_NEAR + 4 * h, near_out.at[h], near_in.at[h]))
     scale_grads()
-    head_copies = [head_part(0), head_part(1)]
     mine_rows = []
     class_copies = []
     for h in range(2):
@@ -497,8 +500,8 @@
             )
             for d in (2, 1, 3)
         ])
-    head_copies += [head_part(2), head_part(3), head_part(4)]
-    for copy in started[: -2 * 3]:
+    head_copies = [head_part(i) for i in range(5)]
+    for copy in started[gathered : -2 * 3]:
         copy.wait_send()
     for q in range(REP):
         losses_ref[q] = jnp.sum(between(scales[2 * q, 1:2] + scales[2 * q + 1, 1:2], CHUNK))
@@ -526,9 +529,9 @@
     head_in, hidden_in, losses_in, head_ref, hidden_ref, losses_ref,
     head, hidden, losses, in_sem, out_sem,
 ):
-    rows = FEAT // 4
+    rows = FEAT // 8
     moves = [(hidden_in, hidden, hidden_ref), (losses_in, losses, losses_ref)]
-    for i in range(4):
+    for i in range(8):
         at = pl.ds(i * rows, rows)
         moves.append((head_in.at[at], head.at[at], head_ref.at[at]))
     loads = [pltpu.make_async_copy(m[0], m[1], in_sem.at[i]) for i, m in enumerate(moves)]
@@ -614,8 +617,8 @@
             pltpu.VMEM((FEAT, COLS), BF16),
             pltpu.VMEM((1, TOK, FEAT), BF16),
             pltpu.SMEM((REP,), F32),
-            pltpu.SemaphoreType.DMA((6,)),
-            pltpu.SemaphoreType.DMA((6,)),
+            pltpu.SemaphoreType.DMA((10,)),
+            pltpu.SemaphoreType.DMA((10,)),
         ],
         compiler_params=pltpu.CompilerParams(vmem_limit_bytes=limit),
     )(*results)

time: 73.6 us -> 73.7 us (level)
  no operation moved by 1% of the time
where the time goes in v6:
time: 73.7 us; the launch traced here: 73.6 us
  Pallas kernels  72.9 us (99%)
    pallas_call x1, Pallas kernels, shards(): pl.pallas_call(kernel, out_shape=shapes, in_specs=[hbm] * 6, out_specs=(h...  70.7 us
    pallas_call x1, Pallas kernels, shards(): pl.pallas_call(hand_over, out_shape=shapes, in_specs=[hbm] * 3, out_specs...  2.25 us

profile of v6, /device:TPU:1, one launch (start us, length us, event | category | flops | bytes accessed | tf_op | source)
XLA Modules:
  0.0 73.6 jit_solution(3866029049943592269)
XLA Ops:
  0.6 70.7 %shard_map.85 = (bf16[512,1280]{1,0:T(8,128)(2,1)}, bf16[1,64,512]{2,1,0:T(8,128)(2,1)}, f32[4]{0:T(128)}) custom-call(s32[4]{0:T(128)} %counts_hbm.1, f32[4]{0:T(128)} %cot_hbm.1, s32[4,64]{1,0:T(4,128)} %positions_hbm.1, s32[4,64]{1,0:T(4,128)} %targets_hbm.1, bf16[1,64,512]{2,1,0:T(8,128)(2,1)} %hidden_hbm.1, bf16[512,1280]{1,0:T(8,128)(2,1)} %weight_hbm.1), custom_call_target="tpu_custom_call" | custom-call | flops 1006632960 | bytes 2621440 | tf_op jit(solution)/shard_map/pallas_call | solution.py:558
  71.3 2.2 %shard_map.86 = (bf16[512,1280]{1,0:T(8,128)(2,1)}, bf16[1,64,512]{2,1,0:T(8,128)(2,1)}, f32[4]{0:T(128)}) custom-call(bf16[512,1280]{1,0:T(8,128)(2,1)} %get-tuple-element.6.head_in, bf16[1,64,512]{2,1,0:T(8,128)(2,1)} %get-tuple-element.7.hidden_in, f32[4]{0:T(128)} %get-tuple-element.8.losses_in), custom_call_target="tpu_custom_call" | custom-call | tf_op jit(solution)/shard_map/pallas_call | solution.py:611

commit v7 on v5

--- a/solution.py
+++ b/solution.py
@@ -19,23 +19,24 @@
 CHUNK = 32
 HALF = 16
 WIDE = FEAT // 2
+THIN = FEAT // 4
 SPAN = COLS // 2
 
 PICK_CLASS = 0
-PICK_NEAR = 6
-PICK_REP = 14
-LOGIT_CORE = 20
-LOGIT_Y = 28
-STAT_SEQ = 40
-STAT_REP = 55
-GRAD_Y = 58
-GRAD_CORE = 66
-SCALE = 69
-ROW_REP = 76
-ROW_NEAR = 82
-ROW_CLASS = 90
-TARGET_REP = 96
-MESSAGES = 99
+PICK_NEAR = 12
+PICK_REP = 28
+LOGIT_CORE = 40
+LOGIT_Y = 48
+STAT_SEQ = 60
+STAT_REP = 75
+GRAD_Y = 78
+GRAD_CORE = 86
+SCALE = 89
+ROW_REP = 96
+ROW_NEAR = 108
+ROW_CLASS = 124
+TARGET_REP = 136
+MESSAGES = 139
 
 
 def iota(shape, dim):
@@ -182,8 +183,8 @@
         jnp.where(pick_at, 1.0, 0.0).astype(BF16), hidden_ref[0], preferred_element_type=F32
     )
     folded = fold_rows(own_rows).astype(BF16)
-    for h in range(2):
-        pick_class[h, member] = folded[:, h * WIDE : (h + 1) * WIDE]
+    for h in range(4):
+        pick_class[h, member] = folded[:, h * THIN : (h + 1) * THIN]
 
     pl.semaphore_wait(barrier, len(friends))
 
@@ -195,7 +196,7 @@
             )
             for d in (2, 1, 3)
         ]
-        for h in range(2)
+        for h in range(4)
     ]
 
     def send_near(number, src, dst):
@@ -229,10 +230,10 @@
 
     totals = []
     near_copies = []
-    for h in range(2):
+    for h in range(4):
         for copy in class_copies[h]:
             copy.wait_recv()
-        total = jnp.zeros((SLOTS, WIDE), F32)
+        total = jnp.zeros((SLOTS, THIN), F32)
         for j in range(4):
             block = unfold_rows(pick_class[h, j].astype(F32))
             total = total + jnp.where(owner_col == cls + 4 * j, block, 0.0)
@@ -241,7 +242,7 @@
         totals.append(total)
     head_at_targets(1)
     rep_copies = []
-    for h in range(2):
+    for h in range(4):
         for copy in near_copies[h]:
             copy.wait_recv()
         total = totals[h]
@@ -254,18 +255,20 @@
         ])
 
     def partial_logits(h, core, k):
-        rows = picked[h, pl.ds(2 * core, 2)].reshape(2 * SLOTS, WIDE)
+        rows = jnp.concatenate(
+            [picked[2 * h + i, pl.ds(2 * core, 2)].reshape(2 * SLOTS, THIN) for i in range(2)], axis=1
+        )
         return jnp.dot(
             rows, weight[h * WIDE : (h + 1) * WIDE, k * SPAN : (k + 1) * SPAN],
             preferred_element_type=F32,
         ).reshape(4, CHUNK, SPAN)
 
-    for copy in rep_copies[0]:
+    for copy in rep_copies[0] + rep_copies[1]:
         copy.wait_recv()
     for k in range(2):
         core_out[k] = partial_logits(0, 1 - c, k)
         part[k] = partial_logits(0, c, k)
-    for copy in rep_copies[1]:
+    for copy in rep_copies[2] + rep_copies[3]:
         copy.wait_recv()
     order = (2, 1, 3, 0)
     core_copies = []
@@ -316,8 +319,8 @@
         fwd_copies[k][1].wait_recv()
         y_sum[k, 1] = y_fwd[k, 1] + part[k, y_plus(3), HALF:CHUNK]
         last_copies.append(send(number + 5, y_sum.at[k, 1], y_acc.at[k, 1], at_y(3)))
-    for h in range(2):
-        picked_t[h * WIDE : (h + 1) * WIDE] = picked[h].reshape(REP * SLOTS, WIDE).T
+    for h in range(4):
+        picked_t[h * THIN : (h + 1) * THIN] = picked[h].reshape(REP * SLOTS, THIN).T
     for copy in last_copies:
         copy.wait_recv()
     for k in range(2):
@@ -376,7 +379,10 @@
         )
         for n, i in enumerate(chunks):
             row_sums[h, i] = rows[n * CHUNK : (n + 1) * CHUNK]
-            row_out[h, i] = rows[n * CHUNK : (n + 1) * CHUNK].astype(BF16)
+            for p in range(2):
+                row_out[2 * h + p, i] = rows[
+                    n * CHUNK : (n + 1) * CHUNK, p * THIN : (p + 1) * THIN
+                ].astype(BF16)
 
     for h in range(2):
         head_times(h, [4 * c + y_plus(i) for i in (0, 1, 3)])
@@ -395,13 +401,14 @@
     rep_copies = []
     for h in range(2):
         head_times(h, [4 * c + y_plus(2), 4 * (1 - c) + y_plus(2)])
-        rep_copies.append([
-            send(
-                ROW_REP + 3 * h + d - 1, row_out.at[h, pl.ds(2 * lax.rem(x + d, REP), 2)],
-                row_in.at[h, d - 1], at_x(d),
-            )
-            for d in (2, 1, 3)
-        ])
+        for p in (2 * h, 2 * h + 1):
+            rep_copies.append([
+                send(
+                    ROW_REP + 3 * p + d - 1, row_out.at[p, pl.ds(2 * lax.rem(x + d, REP), 2)],
+                    row_in.at[p, d - 1], at_x(d),
+                )
+                for d in (2, 1, 3)
+            ])
 
     for copy in stat_copies:
         copy.wait_recv()
@@ -445,7 +452,9 @@
         column_sum = target_out[x, h].astype(F32)
         for i in range(3):
             column_sum = column_sum + target_in[i, h].astype(F32)
-        owns.append(slot_target * column_sum + slot_factors[0] * row_sums[h, pl.ds(2 * x, 2)].reshape(SLOTS, WIDE))
+        rows = row_sums[h, pl.ds(2 * x, 2)].reshape(SLOTS, WIDE)
+        own = slot_target * column_sum + slot_factors[0] * rows
+        owns += [own[:, 0:THIN], own[:, THIN:WIDE]]
 
     def scale_grads():
         for i in range(8):
@@ -467,24 +476,24 @@
         return copy
 
     near_copies = []
-    for h in range(2):
+    for h in range(4):
         for copy in rep_copies[h]:
             copy.wait_recv()
         for i in range(3):
-            owns[h] = owns[h] + slot_factors[i + 1] * row_in[h, i].reshape(SLOTS, WIDE).astype(F32)
+            owns[h] = owns[h] + slot_factors[i + 1] * row_in[h, i].reshape(SLOTS, THIN).astype(F32)
         near_out[h] = owns[h].astype(BF16)
         near_copies.append(send_near(ROW_NEAR + 4 * h, near_out.at[h], near_in.at[h]))
     scale_grads()
     head_copies = [head_part(0), head_part(1)]
     mine_rows = []
     class_copies = []
-    for h in range(2):
+    for h in range(4):
         for copy in near_copies[h]:
             copy.wait_recv()
         own = owns[h]
         for i in range(3):
             own = own + near_in[h, i].astype(F32)
-        mine = jnp.zeros((FOLD, WIDE), F32)
+        mine = jnp.zeros((FOLD, THIN), F32)
         for j in range(4):
             block = fold_rows(jnp.where(owner_col == cls + 4 * j, own, 0.0))
             class_out[h, j] = block.astype(BF16)
@@ -498,14 +507,14 @@
             for d in (2, 1, 3)
         ])
     head_copies += [head_part(2), head_part(3), head_part(4)]
-    for copy in started[: -2 * 3]:
+    for copy in started[: -4 * 3]:
         copy.wait_send()
     for q in range(REP):
         losses_ref[q] = jnp.sum(between(scales[2 * q, 1:2] + scales[2 * q + 1, 1:2], CHUNK))
     for copy in head_copies:
         copy.wait()
     put = jnp.where(put_at, 1.0, 0.0).astype(BF16)
-    for h in range(2):
+    for h in range(4):
         for copy in class_copies[h]:
             copy.wait_recv()
         mine = mine_rows[h]
@@ -513,7 +522,7 @@
             mine = mine + class_in[h, i].astype(F32)
         final = unfold_rows(mine.astype(BF16).astype(F32))
         final = jnp.where(owner_col == z, final, 0.0).astype(BF16)
-        grad_ref[0, :, h * WIDE : (h + 1) * WIDE] = jnp.dot(
+        grad_ref[0, :, h * THIN : (h + 1) * THIN] = jnp.dot(
             put, final, preferred_element_type=F32
         ).astype(BF16)
 
@@ -564,10 +573,10 @@
             pltpu.VMEM((REP, SLOTS), jnp.int32),
             pltpu.VMEM((1, TOK, FEAT), BF16),
             pltpu.VMEM((FEAT, COLS), BF16),
-            pltpu.VMEM((2, 4, FOLD, WIDE), BF16),
-            pltpu.VMEM((2, SLOTS, WIDE), BF16),
-            pltpu.VMEM((2, 3, SLOTS, WIDE), BF16),
-            pltpu.VMEM((2, REP, SLOTS, WIDE), BF16),
+            pltpu.VMEM((4, 4, FOLD, THIN), BF16),
+            pltpu.VMEM((4, SLOTS, THIN), BF16),
+            pltpu.VMEM((4, 3, SLOTS, THIN), BF16),
+            pltpu.VMEM((4, REP, SLOTS, THIN), BF16),
             pltpu.VMEM((FEAT, REP * SLOTS), BF16),
             pltpu.VMEM((8, CHUNK, 1), jnp.int32),
             pltpu.VMEM((REP, 2, SLOTS, WIDE), BF16),
@@ -586,12 +595,12 @@
             pltpu.VMEM((2 * REP, CHUNK, COLS), BF16),
             pltpu.VMEM((2 * REP, CHUNK, COLS), BF16),
             pltpu.VMEM((2, 2 * REP, CHUNK, WIDE), F32),
-            pltpu.VMEM((2, 2 * REP, CHUNK, WIDE), BF16),
-            pltpu.VMEM((2, 3, 2, CHUNK, WIDE), BF16),
-            pltpu.VMEM((2, SLOTS, WIDE), BF16),
-            pltpu.VMEM((2, 3, SLOTS, WIDE), BF16),
-            pltpu.VMEM((2, 4, FOLD, WIDE), BF16),
-            pltpu.VMEM((2, 3, FOLD, WIDE), BF16),
+            pltpu.VMEM((4, 2 * REP, CHUNK, THIN), BF16),
+            pltpu.VMEM((4, 3, 2, CHUNK, THIN), BF16),
+            pltpu.VMEM((4, SLOTS, THIN), BF16),
+            pltpu.VMEM((4, 3, SLOTS, THIN), BF16),
+            pltpu.VMEM((4, 4, FOLD, THIN), BF16),
+            pltpu.VMEM((4, 3, FOLD, THIN), BF16),
             pltpu.VMEM((FEAT, COLS), BF16),
             pltpu.SemaphoreType.DMA((MESSAGES,)),
             pltpu.SemaphoreType.DMA((MESSAGES,)),

time: 73.6 us -> 73.9 us (level)
  no operation moved by 1% of the time
where the time goes in v7:
time: 73.9 us; the launch traced here: 73.8 us
  Pallas kernels  73.1 us (99%)
    pallas_call x1, Pallas kernels, shards(): pl.pallas_call(kernel, out_shape=shapes, in_specs=[hbm] * 6, out_specs=(h...  70.9 us
    pallas_call x1, Pallas kernels, shards(): pl.pallas_call(hand_over, out_shape=shapes, in_specs=[hbm] * 3, out_specs...  2.16 us

profile of v7, /device:TPU:1, one launch (start us, length us, event | category | flops | bytes accessed | tf_op | source)
XLA Modules:
  0.0 73.8 jit_solution(7133714928541448258)
XLA Ops:
  0.6 70.9 %shard_map.85 = (bf16[512,1280]{1,0:T(8,128)(2,1)}, bf16[1,64,512]{2,1,0:T(8,128)(2,1)}, f32[4]{0:T(128)}) custom-call(s32[4]{0:T(128)} %counts_hbm.1, f32[4]{0:T(128)} %cot_hbm.1, s32[4,64]{1,0:T(4,128)} %positions_hbm.1, s32[4,64]{1,0:T(4,128)} %targets_hbm.1, bf16[1,64,512]{2,1,0:T(8,128)(2,1)} %hidden_hbm.1, bf16[512,1280]{1,0:T(8,128)(2,1)} %weight_hbm.1), custom_call_target="tpu_custom_call" | custom-call | flops 1006632960 | bytes 2621440 | tf_op jit(solution)/shard_map/pallas_call | solution.py:564
  71.6 2.2 %shard_map.86 = (bf16[512,1280]{1,0:T(8,128)(2,1)}, bf16[1,64,512]{2,1,0:T(8,128)(2,1)}, f32[4]{0:T(128)}) custom-call(bf16[512,1280]{1,0:T(8,128)(2,1)} %get-tuple-element.6.head_in, bf16[1,64,512]{2,1,0:T(8,128)(2,1)} %get-tuple-element.7.hidden_in, f32[4]{0:T(128)} %get-tuple-element.8.losses_in), custom_call_target="tpu_custom_call" | custom-call | tf_op jit(solution)/shard_map/pallas_call | solution.py:617

commit v8 on v5

--- a/solution.py
+++ b/solution.py
@@ -392,6 +392,30 @@
         head_times(h, [4 * (1 - c) + y_plus(i) for i in (0, 1, 3)])
     for copy in relays:
         copy.wait_recv()
+    def send_scales():
+        for copy in stat_copies:
+            copy.wait_recv()
+        total_max, total_sum, target_logit = merge_stats(stat_rep, REP)
+        lane = iota((1, 128), 1)
+        live = (lane < CHUNK) & (lane + first_slot < my_count)
+        count_row = jnp.full((1, 128), my_count.astype(F32), F32)
+        weight_row = jnp.where(live, jnp.full((1, 128), my_cot, F32) / count_row, 0.0)
+        factor_row = jnp.zeros((1, 128), F32)
+        for i in range(REP):
+            there = jnp.exp(turn(stat_rep[i], 3 * CHUNK) - total_max) / total_sum
+            factor = jnp.where(live, weight_row * there, 0.0)
+            factor_row = factor_row + (turn(factor, 128 - i * CHUNK) if i else factor)
+        at_target = jnp.where(
+            live, weight_row * (jnp.exp(target_logit - total_max) / total_sum - 1.0), 0.0
+        )
+        row_loss = jnp.where(live, (jnp.log(total_sum) + total_max - target_logit) / count_row, 0.0)
+        scales[my_chunk, 0:1] = factor_row
+        scales[my_chunk, 1:2] = at_target + turn(row_loss, 128 - CHUNK)
+        return [
+            send(SCALE + d - 1, scales.at[my_chunk], scales.at[my_chunk], {"vocab": lax.rem(v + d, 8)})
+            for d in range(1, 8)
+        ]
+
     rep_copies = []
     for h in range(2):
         head_times(h, [4 * c + y_plus(2), 4 * (1 - c) + y_plus(2)])
@@ -402,29 +426,9 @@
             )
             for d in (2, 1, 3)
         ])
-
-    for copy in stat_copies:
-        copy.wait_recv()
-    total_max, total_sum, target_logit = merge_stats(stat_rep, REP)
-    lane = iota((1, 128), 1)
-    live = (lane < CHUNK) & (lane + first_slot < my_count)
-    count_row = jnp.full((1, 128), my_count.astype(F32), F32)
-    weight_row = jnp.where(live, jnp.full((1, 128), my_cot, F32) / count_row, 0.0)
-    factor_row = jnp.zeros((1, 128), F32)
-    for i in range(REP):
-        there = jnp.exp(turn(stat_rep[i], 3 * CHUNK) - total_max) / total_sum
-        factor = jnp.where(live, weight_row * there, 0.0)
-        factor_row = factor_row + (turn(factor, 128 - i * CHUNK) if i else factor)
-    at_target = jnp.where(
-        live, weight_row * (jnp.exp(target_logit - total_max) / total_sum - 1.0), 0.0
-    )
-    row_loss = jnp.where(live, (jnp.log(total_sum) + total_max - target_logit) / count_row, 0.0)
-    scales[my_chunk, 0:1] = factor_row
-    scales[my_chunk, 1:2] = at_target + turn(row_loss, 128 - CHUNK)
-    scale_copies = [
-        send(SCALE + d - 1, scales.at[my_chunk], scales.at[my_chunk], {"vocab": lax.rem(v + d, 8)})
-        for d in range(1, 8)
-    ]
+        if h == 0:
+            scale_copies = send_scales()
+
     for copy in scale_copies:
         copy.wait_recv()
 

time: 73.6 us -> 74.2 us (level)
  no operation moved by 1% of the time
where the time goes in v8:
time: 74.2 us; the launch traced here: 74.1 us
  Pallas kernels  73.4 us (99%)
    pallas_call x1, Pallas kernels, shards(): pl.pallas_call(kernel, out_shape=shapes, in_specs=[hbm] * 6, out_specs=(h...  71.3 us
    pallas_call x1, Pallas kernels, shards(): pl.pallas_call(hand_over, out_shape=shapes, in_specs=[hbm] * 3, out_specs...  2.16 us

profile of v8, /device:TPU:1, one launch (start us, length us, event | category | flops | bytes accessed | tf_op | source)
XLA Modules:
  0.0 74.1 jit_solution(15822215851728379004)
XLA Ops:
  0.6 71.3 %shard_map.85 = (bf16[512,1280]{1,0:T(8,128)(2,1)}, bf16[1,64,512]{2,1,0:T(8,128)(2,1)}, f32[4]{0:T(128)}) custom-call(s32[4]{0:T(128)} %counts_hbm.1, f32[4]{0:T(128)} %cot_hbm.1, s32[4,64]{1,0:T(4,128)} %positions_hbm.1, s32[4,64]{1,0:T(4,128)} %targets_hbm.1, bf16[1,64,512]{2,1,0:T(8,128)(2,1)} %hidden_hbm.1, bf16[512,1280]{1,0:T(8,128)(2,1)} %weight_hbm.1), custom_call_target="tpu_custom_call" | custom-call | flops 1006632960 | bytes 2621440 | tf_op jit(solution)/shard_map/pallas_call | solution.py:559
  71.9 2.2 %shard_map.86 = (bf16[512,1280]{1,0:T(8,128)(2,1)}, bf16[1,64,512]{2,1,0:T(8,128)(2,1)}, f32[4]{0:T(128)}) custom-call(bf16[512,1280]{1,0:T(8,128)(2,1)} %get-tuple-element.6.head_in, bf16[1,64,512]{2,1,0:T(8,128)(2,1)} %get-tuple-element.7.hidden_in, f32[4]{0:T(128)} %get-tuple-element.8.losses_in), custom_call_target="tpu_custom_call" | custom-call | tf_op jit(solution)/shard_map/pallas_call | solution.py:612
